TPU v7x, 32 devices: a whole 2x2x4 slice. The times are simulated.
32 devices in a mesh: dp: 4 (over x, core), expert: 8 (over z, y).
Axes of the slice: x: 2, y: 2, z: 4, core: 2. Of those that a mesh axis runs over, the one named last changes fastest.
Arguments:
- tokens: bfloat16 [16384, 768], P(('dp', 'expert')), may hold values from -6 to 6
- cotangent: bfloat16 [16384, 768], P(('dp', 'expert')), may hold values from -6 to 6
- expert_ids: int32 [16384, 1], P(('dp', 'expert')), may hold values from 0 to 7
- loss_weights: int32 [8], replicated, may hold values from 1 to 4
- section: int32 [8], replicated, may hold values from 0 to 1, as said below
- norm_gains: float32 [4, 768], replicated, may hold values from 0.5 to 1.5
- attn_qkv: bfloat16 [2, 768, 2304], replicated, may hold values from -0.21875 to 0.21875
- attn_out: bfloat16 [2, 768, 768], replicated, may hold values from -1.25 to 1.25
- ffn_up: bfloat16 [768, 3072], replicated, may hold values from -0.21875 to 0.21875
- ffn_down: bfloat16 [3072, 768], replicated, may hold values from -0.21875 to 0.21875
- expert_up: bfloat16 [8, 768, 3072], P('expert'), may hold values from -0.21875 to 0.21875
- expert_down: bfloat16 [8, 3072, 768], P('expert'), may hold values from -0.3125 to 0.3125
- router: float32 [768, 8], replicated, may hold values from -0.15625 to 0.15625
Outputs:
- block_one: bfloat16 [16384, 768], P(('dp', 'expert'))
- block_two: bfloat16 [16384, 768], P(('dp', 'expert'))
- input_grad: float32 [16384, 768], P(('dp', 'expert'))
- balance_loss: float32 [], replicated
- gains_grad: float32 [4, 768], replicated
- qkv_grad: float32 [2, 768, 2304], P(None, 'expert')
- out_grad: float32 [2, 768, 768], P(None, 'expert')
- up_grad: float32 [768, 3072], P('expert')
- down_grad: float32 [3072, 768], P('expert')
- expert_up_grad: float32 [8, 768, 3072], P('expert', 'dp')
- expert_down_grad: float32 [8, 3072, 768], P('expert', 'dp')
- router_grad: float32 [768, 8], replicated
Inputs may be any that keep to these rules, and one draw needn't show every extreme that they name: `expert_ids`: every expert is named by some token. `section`: some sequences have 0 and some have 1.
All inputs are finite; a program needn't handle non-finite values.
Results may differ from a plain program's by a relative error of at most 0.02.
Values may be sent and summed in bfloat16 or wider, within the bound.
A program may use at most 704 MiB of HBM per device.

v0:
```python
import jax
import jax.numpy as jnp
from jax import lax
from jax.sharding import PartitionSpec as P

H = 12
HD = 64


eps_norm = 1e-05
balance_rate = 1.0
bfloat = jnp.bfloat16
single = jnp.float32
highest = lax.Precision.HIGHEST


def norm_forward(stream, gain):
    centre = jnp.mean(stream, axis=-1, keepdims=True)
    centered = stream - centre
    spread = jnp.mean(centered * centered, axis=-1, keepdims=True)
    factor = lax.rsqrt(spread + eps_norm)
    normed = centered * factor
    return (normed * gain, normed, factor)


def norm_backward(upstream, normed, factor, gain):
    grad_normed = upstream * gain
    inner = jnp.mean(grad_normed * normed, axis=-1, keepdims=True)
    centre = jnp.mean(grad_normed, axis=-1, keepdims=True)
    return (factor * (grad_normed - centre - normed * inner), jnp.sum(upstream * normed, axis=0))


def gelu_tanh(hidden):
    return jax.nn.gelu(hidden, approximate=True)


def gelu_back(hidden, upstream):
    return jax.vjp(gelu_tanh, hidden)[1](upstream)[0]


def masked_scores(query_rows, keys, first, offset):
    rows_block = query_rows.shape[0]
    scores = jnp.einsum("qhd,khd->hqk", query_rows, keys, preferred_element_type=single) * HD ** (
        -0.5
    )
    key_place = jnp.arange(keys.shape[0])
    query_place = offset + first + jnp.arange(rows_block)
    allowed = key_place[None, :] <= query_place[:, None]
    return jnp.where(allowed[None], scores, -1e30)


def attend_forward(queries, keys, values, offset):
    row_count = queries.shape[0]
    rows_block = min(512, row_count)

    def one_block(first):
        scores = masked_scores(queries, keys, first, offset)
        largest = jnp.max(scores, axis=-1, keepdims=True)
        weights = jnp.exp(scores - largest)
        weight_sum = jnp.sum(weights, axis=-1, keepdims=True)
        probs = (weights / weight_sum).astype(bfloat)
        mixed = jnp.einsum("hqk,khd->qhd", probs, values, preferred_element_type=single)
        return (mixed.astype(bfloat), (largest + jnp.log(weight_sum))[..., 0])

    starts = jnp.arange(row_count // rows_block, dtype=jnp.int32) * rows_block
    mixed, log_sums = lax.map(one_block, starts)
    return (mixed.reshape(row_count, H * HD), log_sums)


def attend_backward(queries, keys, values, offset, log_sums, grad_mixed):
    row_count = queries.shape[0]
    key_count = keys.shape[0]
    rows_block = min(512, row_count)
    grad_heads = grad_mixed.reshape(row_count, H, HD)

    def one_block(carry_state, item):
        key_grad, value_grad = carry_state
        first, log_block = item
        scores = masked_scores(queries, keys, first, offset)
        probs = jnp.exp(scores - log_block[..., None])
        grad_probs = jnp.einsum("qhd,khd->hqk", grad_heads, values, preferred_element_type=single)
        inner = jnp.sum(probs * grad_probs, axis=-1, keepdims=True)
        grad_scores = (probs * (grad_probs - inner)).astype(bfloat)
        query_grad = jnp.einsum(
            "hqk,khd->qhd", grad_scores, keys, preferred_element_type=single
        ) * HD ** (-0.5)
        key_grad = key_grad + jnp.einsum(
            "hqk,qhd->khd", grad_scores, queries, preferred_element_type=single
        ) * HD ** (-0.5)
        value_grad = value_grad + jnp.einsum(
            "hqk,qhd->khd", probs.astype(bfloat), grad_heads, preferred_element_type=single
        )
        return ((key_grad, value_grad), query_grad)

    starts = jnp.arange(row_count // rows_block, dtype=jnp.int32) * rows_block
    zeros = jnp.zeros((key_count, H, HD), single)
    (key_grad, value_grad), query_grad = lax.scan(one_block, (zeros, zeros), (starts, log_sums))
    return (
        query_grad.reshape(row_count, H * HD),
        key_grad.reshape(key_count, H * HD),
        value_grad.reshape(key_count, H * HD),
    )


def attention_forward(stream, gain, w_qkv, w_out, offset):
    row_count, model_width = stream.shape
    normed_out, normed, factor = norm_forward(stream, gain)
    normed_low = normed_out.astype(bfloat)
    packed = jnp.dot(normed_low, w_qkv, preferred_element_type=single).astype(bfloat)
    gathered = lax.all_gather(packed[:, model_width:], "dp", axis=0, tiled=True)
    key_count = gathered.shape[0]
    queries = packed[:, :model_width].reshape(row_count, H, HD)
    keys = gathered[:, :model_width].reshape(key_count, H, HD)
    values = gathered[:, model_width:].reshape(key_count, H, HD)
    mixed, log_sums = attend_forward(queries, keys, values, offset)
    branch = jnp.dot(mixed, w_out, preferred_element_type=single)
    saved = (normed, factor, normed_low, queries, keys, values, log_sums, mixed)
    return (stream + branch, saved)


def attention_backward(upstream, saved, gain, w_qkv, w_out, offset):
    normed, factor, normed_low, queries, keys, values, log_sums, mixed = saved
    branch_low = upstream.astype(bfloat)
    out_weight_grad = jnp.dot(mixed.T, branch_low, preferred_element_type=single)
    grad_mixed = jnp.dot(branch_low, w_out.T, preferred_element_type=single).astype(bfloat)
    query_grad, key_grad, value_grad = attend_backward(
        queries, keys, values, offset, log_sums, grad_mixed
    )
    all_grads = jnp.concatenate([key_grad, value_grad], axis=1)
    own_grads = lax.psum_scatter(
        all_grads.astype(jnp.bfloat16), "dp", scatter_dimension=0, tiled=True
    ).astype(jnp.float32)
    packed_grad = jnp.concatenate([query_grad, own_grads], axis=1).astype(bfloat)
    qkv_weight_grad = jnp.dot(normed_low.T, packed_grad, preferred_element_type=single)
    normed_grad = jnp.dot(packed_grad, w_qkv.T, preferred_element_type=single)
    stream_grad, gain_grad = norm_backward(normed_grad, normed, factor, gain)
    return (upstream + stream_grad, gain_grad, qkv_weight_grad, out_weight_grad)


def routing(expert_ids, expert_count, capacity):
    indices = expert_ids[:, 0]
    one_hot = (indices[:, None] == jnp.arange(expert_count, dtype=jnp.int32)[None, :]).astype(
        jnp.int32
    )
    earlier = jnp.cumsum(one_hot, axis=0) - one_hot
    slots = jnp.sum(earlier * one_hot, axis=1)
    kept_rows = slots < capacity
    target = jnp.where(kept_rows, indices * capacity + slots, expert_count * capacity)
    return (one_hot.astype(single), target, kept_rows)


def body(
    tokens,
    cotangent,
    expert_ids,
    loss_weights,
    section,
    norm_gains,
    attn_qkv,
    attn_out,
    ffn_up,
    ffn_down,
    expert_up,
    expert_down,
    router,
):
    row_count, model_width = tokens.shape
    expert_count = router.shape[1]
    capacity = 5 * row_count // (4 * expert_count)
    slots_all = expert_count * capacity
    group_count = lax.axis_size("expert")
    total_tokens = row_count * lax.axis_size("dp") * group_count
    offset = lax.axis_index("dp") * row_count
    sequence = lax.axis_index("expert")
    switch = section[sequence].astype(single)
    seq_weight = loss_weights[sequence].astype(single)
    inputs = tokens.astype(single)
    first_stream, saved_one = attention_forward(
        inputs, norm_gains[0], attn_qkv[0], attn_out[0], offset
    )
    ffn_out, ffn_normed, ffn_factor = norm_forward(first_stream, norm_gains[1])
    ffn_low = ffn_out.astype(bfloat)
    hidden = jnp.dot(ffn_low, ffn_up, preferred_element_type=single)
    acts_low = gelu_tanh(hidden).astype(bfloat)
    block_out = first_stream + jnp.dot(acts_low, ffn_down, preferred_element_type=single)
    second_stream, saved_two = attention_forward(
        block_out, norm_gains[2], attn_qkv[1], attn_out[1], offset
    )
    moe_in, moe_normed, moe_factor = norm_forward(second_stream, norm_gains[3])
    logits = jnp.dot(moe_in, router, precision=highest)
    one_hot, target, kept_rows = routing(expert_ids, expert_count, capacity)
    gates = jax.nn.sigmoid(jnp.sum(logits * one_hot, axis=1))
    outgoing = (
        jnp.zeros((slots_all, model_width), bfloat)
        .at[target]
        .set(moe_in.astype(bfloat), mode="drop")
    )
    arrived = lax.all_to_all(
        outgoing.reshape(expert_count, capacity, model_width),
        "expert",
        split_axis=0,
        concat_axis=0,
        tiled=True,
    )
    expert_rows = arrived.reshape(-1, model_width)
    expert_hidden = jnp.dot(expert_rows, expert_up[0], preferred_element_type=single)
    expert_acts = gelu_tanh(expert_hidden).astype(bfloat)
    expert_result = jnp.dot(expert_acts, expert_down[0], preferred_element_type=single).astype(
        bfloat
    )
    returned = lax.all_to_all(
        expert_result.reshape(group_count, capacity, model_width),
        "expert",
        split_axis=0,
        concat_axis=0,
        tiled=True,
    )
    safe_target = jnp.minimum(target, slots_all - 1)
    kept_float = kept_rows.astype(single)[:, None]
    moe_out = returned.reshape(slots_all, model_width)[safe_target].astype(single) * kept_float
    final = second_stream + gates[:, None] * moe_out
    counts, gate_sums = lax.psum(
        (jnp.sum(one_hot, axis=0), switch * jnp.sum(one_hot * gates[:, None], axis=0)),
        ("dp", "expert"),
    )
    mean_load = total_tokens / expert_count
    coef = (counts - mean_load) / mean_load
    load_balance = jnp.sum(coef * gate_sums) * (balance_rate / total_tokens)
    final_grad = cotangent.astype(single) * seq_weight
    gate_slope = gates * (1.0 - gates)
    gate_grad = jnp.sum(final_grad * moe_out, axis=1)
    balance_term = switch * (balance_rate / total_tokens) * jnp.sum(one_hot * coef[None, :], axis=1)
    logit_grad = (gate_grad + balance_term) * gate_slope
    result_grad = (final_grad * gates[:, None]).astype(bfloat)
    outgoing_grad = (
        jnp.zeros((slots_all, model_width), bfloat).at[target].set(result_grad, mode="drop")
    )
    grad_rows = lax.all_to_all(
        outgoing_grad.reshape(expert_count, capacity, model_width),
        "expert",
        split_axis=0,
        concat_axis=0,
        tiled=True,
    ).reshape(-1, model_width)
    down_expert_grad = jnp.dot(expert_acts.T, grad_rows, preferred_element_type=single)
    grad_acts = jnp.dot(grad_rows, expert_down[0].T, preferred_element_type=single)
    grad_hidden = gelu_back(expert_hidden, grad_acts).astype(bfloat)
    up_expert_grad = jnp.dot(expert_rows.T, grad_hidden, preferred_element_type=single)
    grad_inputs = jnp.dot(grad_hidden, expert_up[0].T, preferred_element_type=single).astype(bfloat)
    grad_back = lax.all_to_all(
        grad_inputs.reshape(group_count, capacity, model_width),
        "expert",
        split_axis=0,
        concat_axis=0,
        tiled=True,
    )
    moe_in_grad = grad_back.reshape(slots_all, model_width)[safe_target].astype(single) * kept_float
    routed_grad = logit_grad[:, None] * one_hot
    moe_in_grad = moe_in_grad + jnp.dot(routed_grad, router.T, precision=highest)
    router_local = switch * jnp.dot(moe_in.T, routed_grad, precision=highest)
    norm_grad_two, gain_three = norm_backward(moe_in_grad, moe_normed, moe_factor, norm_gains[3])
    second_grad = final_grad + norm_grad_two
    block_grad, gain_two, qkv_two, out_two = attention_backward(
        second_grad, saved_two, norm_gains[2], attn_qkv[1], attn_out[1], offset
    )
    branch_low = block_grad.astype(bfloat)
    down_local = jnp.dot(acts_low.T, branch_low, preferred_element_type=single)
    grad_dense_acts = jnp.dot(branch_low, ffn_down.T, preferred_element_type=single)
    grad_dense_hidden = gelu_back(hidden, grad_dense_acts).astype(bfloat)
    up_local = jnp.dot(ffn_low.T, grad_dense_hidden, preferred_element_type=single)
    ffn_in_grad = jnp.dot(grad_dense_hidden, ffn_up.T, preferred_element_type=single)
    norm_grad_one, gain_one = norm_backward(ffn_in_grad, ffn_normed, ffn_factor, norm_gains[1])
    first_grad = block_grad + norm_grad_one
    input_grad, gain_zero, qkv_one, out_one = attention_backward(
        first_grad, saved_one, norm_gains[0], attn_qkv[0], attn_out[0], offset
    )
    expert_up_part, expert_down_part = (
        lax.psum_scatter(
            up_expert_grad[None].astype(jnp.bfloat16), "dp", scatter_dimension=1, tiled=True
        ).astype(jnp.float32),
        lax.psum_scatter(
            down_expert_grad[None].astype(jnp.bfloat16), "dp", scatter_dimension=1, tiled=True
        ).astype(jnp.float32),
    )
    gains_local = jnp.stack([gain_zero, gain_one, gain_two, gain_three])
    gains_total, router_total = lax.psum((gains_local, router_local), ("dp", "expert"))
    qkv_local = jnp.stack([qkv_one, qkv_two])
    out_local = jnp.stack([out_one, out_two])
    qkv_part, out_part, up_part, down_part = (
        lax.psum_scatter(
            qkv_local.astype(jnp.bfloat16), "expert", scatter_dimension=1, tiled=True
        ).astype(jnp.float32),
        lax.psum_scatter(
            out_local.astype(jnp.bfloat16), "expert", scatter_dimension=1, tiled=True
        ).astype(jnp.float32),
        lax.psum_scatter(
            up_local.astype(jnp.bfloat16), "expert", scatter_dimension=0, tiled=True
        ).astype(jnp.float32),
        lax.psum_scatter(
            down_local.astype(jnp.bfloat16), "expert", scatter_dimension=0, tiled=True
        ).astype(jnp.float32),
    )
    qkv_part, out_part, up_part, down_part = (
        lax.psum(qkv_part.astype(jnp.bfloat16), "dp").astype(jnp.float32),
        lax.psum(out_part.astype(jnp.bfloat16), "dp").astype(jnp.float32),
        lax.psum(up_part.astype(jnp.bfloat16), "dp").astype(jnp.float32),
        lax.psum(down_part.astype(jnp.bfloat16), "dp").astype(jnp.float32),
    )
    return (
        block_out.astype(bfloat),
        final.astype(bfloat),
        input_grad,
        load_balance,
        gains_total,
        qkv_part,
        out_part,
        up_part,
        down_part,
        expert_up_part,
        expert_down_part,
        router_total,
    )


def solution(mesh):
    in_specs = (
        P(("dp", "expert"), None),
        P(("dp", "expert"), None),
        P(("dp", "expert"), None),
        P(),
        P(),
        P(),
        P(),
        P(),
        P(),
        P(),
        P("expert", None, None),
        P("expert", None, None),
        P(),
    )
    out_specs = (
        P(("dp", "expert"), None),
        P(("dp", "expert"), None),
        P(("dp", "expert"), None),
        P(),
        P(),
        P(None, "expert", None),
        P(None, "expert", None),
        P("expert", None),
        P("expert", None),
        P("expert", "dp", None),
        P("expert", "dp", None),
        P(),
    )
    return jax.shard_map(body, mesh=mesh, in_specs=in_specs, out_specs=out_specs, check_vma=False)
```

profile of v0, /device:TPU:0, one launch (start us, length us, event | category | flops | bytes accessed | tf_op | source)
XLA Modules:
  0.0 1405.6 jit_solution(9237689064250381162)
XLA Ops:
  18.4 48.1 %all-gather.3.cloned.1.call-done = bf16[2048,1536]{1,0:T(8,128)(2,1)} async-done(((bf16[512,1536]{1,0:T(8,128)(2,1)}), bf16[2048,1536]{1,0:T(8,128)(2,1)}) %all-gather.3.cloned.1.call-update) | async-done | bytes 6291472 | tf_op jit(solution)/shard_map/all_gather | solution.py:110
  82.1 22.3 %fusion.12 = (f32[12,512]{1,0:T(8,128)S(1)}, f32[12,512,2048]{2,1,0:T(8,128)}) fusion(pred[512,2048]{1,0:T(8,128)(4,1)S(1)} %iota_compare_fusion, bf16[512,12,64]{0,2,1:T(8,128)(2,1)S(1)} %bitcast.157, bf16[2048,12,64]{0,2,1:T(8,128)(2,1)} %bitcast.147), kind=kOutput, calls=%fused_computation.26 | convolution fusion | flops 1648355328 | bytes 55336960 | tf_op jit(solution)/shard_map/while/body/eval_jaxpr/qhd,khd->hqk/dot_general | solution.py:43
  104.4 21.9 %fusion = f32[12,512]{1,0:T(8,128)S(1)} fusion(f32[12,512]{1,0:T(8,128)S(1)} %get-tuple-element.149, f32[12,512,2048]{2,1,0:T(8,128)} %get-tuple-element.150, pred[512,2048]{1,0:T(8,128)(4,1)S(1)} %iota_compare_fusion), kind=kLoop, calls=%fused_computation.16 | loop fusion | flops 50325504 | bytes 51429376 | tf_op jit(solution)/shard_map/while/body/eval_jaxpr/reduce_sum | solution.py:60
  126.3 21.1 %fusion.80 = bf16[12,64,512]{2,1,0:T(8,128)(2,1)S(1)} fusion(bf16[2048,12,64]{0,2,1:T(8,128)(2,1)} %bitcast.151, f32[12,512]{1,0:T(8,128)S(1)} %fusion, f32[12,512]{1,0:T(8,128)S(1)} %get-tuple-element.149, f32[12,512,2048]{2,1,0:T(8,128)} %get-tuple-element.150, pred[512,2048]{1,0:T(8,128)(4,1)S(1)} %iota_compare_fusion), kind=kOutput, calls=%fused_computation.141 | convolution fusion | flops 1673920512 | bytes 55361536 | tf_op jit(solution)/shard_map/while/body/eval_jaxpr/hqk,khd->qhd/dot_general | solution.py:62
  167.5 42.9 %all-gather.5.cloned.1.call-done = bf16[2048,1536]{1,0:T(8,128)(2,1)} async-done(((bf16[512,1536]{1,0:T(8,128)(2,1)}), bf16[2048,1536]{1,0:T(8,128)(2,1)}) %all-gather.5.cloned.1.call-update) | async-done | bytes 6291472 | tf_op jit(solution)/shard_map/all_gather | solution.py:110
  225.8 22.3 %fusion.13 = (f32[12,512]{1,0:T(8,128)S(1)}, f32[12,512,2048]{2,1,0:T(8,128)}) fusion(pred[512,2048]{1,0:T(8,128)(4,1)S(1)} %iota_compare_fusion, bf16[512,12,64]{0,2,1:T(8,128)(2,1)S(1)} %bitcast.159, bf16[2048,12,64]{0,2,1:T(8,128)(2,1)} %bitcast.149), kind=kOutput, calls=%fused_computation.27 | convolution fusion | flops 1648355328 | bytes 55336960 | tf_op jit(solution)/shard_map/while/body/eval_jaxpr/qhd,khd->hqk/dot_general | solution.py:43
  248.1 22.0 %fusion.1 = f32[12,512]{1,0:T(8,128)S(1)} fusion(f32[12,512]{1,0:T(8,128)S(1)} %get-tuple-element.155, f32[12,512,2048]{2,1,0:T(8,128)} %get-tuple-element.156, pred[512,2048]{1,0:T(8,128)(4,1)S(1)} %iota_compare_fusion), kind=kLoop, calls=%fused_computation.17 | loop fusion | flops 50325504 | bytes 51429376 | tf_op jit(solution)/shard_map/while/body/eval_jaxpr/reduce_sum | solution.py:60
  270.1 21.2 %fusion.79 = bf16[12,64,512]{2,1,0:T(8,128)(2,1)S(1)} fusion(bf16[2048,12,64]{0,2,1:T(8,128)(2,1)} %bitcast.153, f32[12,512]{1,0:T(8,128)S(1)} %fusion.1, f32[12,512]{1,0:T(8,128)S(1)} %get-tuple-element.155, f32[12,512,2048]{2,1,0:T(8,128)} %get-tuple-element.156, pred[512,2048]{1,0:T(8,128)(4,1)S(1)} %iota_compare_fusion), kind=kOutput, calls=%fused_computation.140 | convolution fusion | flops 1673920512 | bytes 55361536 | tf_op jit(solution)/shard_map/while/body/eval_jaxpr/hqk,khd->qhd/dot_general | solution.py:62
  309.0 18.1 %all-to-all-done = bf16[8,80,768]{2,1,0:T(8,128)(2,1)} async-done(((bf16[8,80,768]{2,1,0:T(8,128)(2,1)}), bf16[8,80,768]{2,1,0:T(8,128)(2,1)}, u32[]{:S(2)}, u32[]{:S(2)}) %all-to-all-start) | async-done | bytes 983072 | tf_op jit(solution)/shard_map/all_to_all | solution.py:198
  390.8 41.5 %psum.56 = f32[8]{0:T(128)S(1)} all-reduce(f32[8]{0:T(128)S(1)} %get-tuple-element.121), channel_id=1, replica_groups=mesh['dp'=4,'expert'=8] {'dp','expert'}, use_global_device_ids=true, to_apply=%region_20.21 | all-reduce | flops 8 | bytes 64 | tf_op jit(solution)/shard_map/psum | solution.py:222
  452.1 22.4 %fusion.46 = bf16[12,64,2048]{2,1,0:T(8,128)(2,1)} fusion(bf16[512,12,64]{0,2,1:T(8,128)(2,1)S(1)} %bitcast.163, f32[12,512]{1,0:T(8,128)S(1)} %log_add_fusion.1, f32[12,512,2048]{2,1,0:T(8,128)} %get-tuple-element.156, pred[512,2048]{1,0:T(8,128)(4,1)S(1)} %iota_compare_fusion), kind=kOutput, calls=%fused_computation.80 | convolution fusion | flops 1662517248 | bytes 55336960 | tf_op jit(solution)/shard_map/while/body/eval_jaxpr/hqk,qhd->khd/dot_general | solution.py:90
  474.5 37.3 %multiply_reduce_fusion.1 = (f32[12,512]{1,0:T(8,128)S(1)}, f32[12,512,2048]{2,1,0:T(8,128)}) fusion(f32[12,512]{1,0:T(8,128)S(1)} %log_add_fusion.1, f32[12,512,2048]{2,1,0:T(8,128)} %get-tuple-element.156, pred[512,2048]{1,0:T(8,128)(4,1)S(1)} %iota_compare_fusion, bf16[512,12,64]{0,2,1:T(8,128)(2,1)S(1)} %bitcast.164, bf16[2048,12,64]{0,2,1:T(8,128)(2,1)} %bitcast.154), kind=kOutput, calls=%fused_computation.8 | convolution fusion | flops 1673521152 | bytes 105693184 | tf_op jit(solution)/shard_map/while/body/eval_jaxpr/qhd,khd->hqk/dot_general | solution.py:81
  511.8 40.3 %multiply_convert_fusion.1 = bf16[12,512,2048]{2,1,0:T(8,128)(2,1)} fusion(f32[12,512,2048]{2,1,0:T(8,128)} %get-tuple-element.161, f32[12,512]{1,0:T(8,128)S(1)} %get-tuple-element.160, f32[12,512]{1,0:T(8,128)S(1)} %log_add_fusion.1, f32[12,512,2048]{2,1,0:T(8,128)} %get-tuple-element.156, pred[512,2048]{1,0:T(8,128)(4,1)S(1)} %iota_compare_fusion), kind=kLoop, calls=%fused_computation.7 | loop fusion | flops 75497472 | bytes 126926848 | tf_op jit(solution)/shard_map/while/body/eval_jaxpr/convert_element_type | solution.py:83
  585.7 41.4 %reduce-scatter.9.cloned.1.call-done = bf16[512,1536]{0,1:T(8,128)(2,1)} async-done(((bf16[2048,1536]{0,1:T(8,128)(2,1)}), bf16[512,1536]{0,1:T(8,128)(2,1)}) %reduce-scatter.9.cloned.1.call-update) | async-done | bytes 1572880 | tf_op jit(solution)/shard_map/reduce_scatter | solution.py:130
  652.5 22.3 %fusion.49 = bf16[12,64,2048]{2,1,0:T(8,128)(2,1)} fusion(bf16[512,12,64]{0,2,1:T(8,128)(2,1)S(1)} %bitcast.165, f32[12,512]{1,0:T(8,128)S(1)} %log_add_fusion, f32[12,512,2048]{2,1,0:T(8,128)} %get-tuple-element.150, pred[512,2048]{1,0:T(8,128)(4,1)S(1)} %iota_compare_fusion), kind=kOutput, calls=%fused_computation.81 | convolution fusion | flops 1662517248 | bytes 55336960 | tf_op jit(solution)/shard_map/while/body/eval_jaxpr/hqk,qhd->khd/dot_general | solution.py:90
  674.8 37.1 %multiply_reduce_fusion = (f32[12,512]{1,0:T(8,128)S(1)}, f32[12,512,2048]{2,1,0:T(8,128)}) fusion(f32[12,512]{1,0:T(8,128)S(1)} %log_add_fusion, f32[12,512,2048]{2,1,0:T(8,128)} %get-tuple-element.150, pred[512,2048]{1,0:T(8,128)(4,1)S(1)} %iota_compare_fusion, bf16[512,12,64]{0,2,1:T(8,128)(2,1)S(1)} %bitcast.166, bf16[2048,12,64]{0,2,1:T(8,128)(2,1)} %bitcast.152), kind=kOutput, calls=%fused_computation.5 | convolution fusion | flops 1673521152 | bytes 105693184 | tf_op jit(solution)/shard_map/while/body/eval_jaxpr/qhd,khd->hqk/dot_general | solution.py:81
  711.9 40.4 %multiply_convert_fusion = bf16[12,512,2048]{2,1,0:T(8,128)(2,1)} fusion(f32[12,512,2048]{2,1,0:T(8,128)} %get-tuple-element.165, f32[12,512]{1,0:T(8,128)S(1)} %get-tuple-element.164, f32[12,512]{1,0:T(8,128)S(1)} %log_add_fusion, f32[12,512,2048]{2,1,0:T(8,128)} %get-tuple-element.150, pred[512,2048]{1,0:T(8,128)(4,1)S(1)} %iota_compare_fusion), kind=kLoop, calls=%fused_computation.4 | loop fusion | flops 75497472 | bytes 126926848 | tf_op jit(solution)/shard_map/while/body/eval_jaxpr/convert_element_type | solution.py:83
  850.1 27.7 %reduce-scatter.21.cloned.1.call-done = bf16[1,192,3072]{2,1,0:T(8,128)(2,1)} async-done(((bf16[1,768,3072]{2,1,0:T(8,128)(2,1)}), bf16[1,192,3072]{2,1,0:T(8,128)(2,1)}) %reduce-scatter.21.cloned.1.call-update) | async-done | bytes 1179664 | tf_op jit(solution)/shard_map/reduce_scatter | solution.py:278
  880.7 70.4 %reduce-scatter.15.cloned.1.call-done = bf16[2,96,768]{2,1,0:T(8,128)(2,1)} async-done(((bf16[2,768,768]{2,1,0:T(8,128)(2,1)}), bf16[2,96,768]{2,1,0:T(8,128)(2,1)}) %reduce-scatter.15.cloned.1.call-update) | async-done | bytes 294928 | tf_op jit(solution)/shard_map/reduce_scatter | solution.py:293
  951.2 98.4 %reduce-scatter.19.cloned.1.call-done = bf16[384,768]{1,0:T(8,128)(2,1)} async-done(((bf16[3072,768]{1,0:T(8,128)(2,1)}), bf16[384,768]{1,0:T(8,128)(2,1)}) %reduce-scatter.19.cloned.1.call-update) | async-done | bytes 589840 | tf_op jit(solution)/shard_map/reduce_scatter | solution.py:299
  1049.6 99.1 %reduce-scatter.17.cloned.1.call-done = bf16[96,3072]{1,0:T(8,128)(2,1)} async-done(((bf16[768,3072]{1,0:T(8,128)(2,1)}), bf16[96,3072]{1,0:T(8,128)(2,1)}) %reduce-scatter.17.cloned.1.call-update) | async-done | bytes 589840 | tf_op jit(solution)/shard_map/reduce_scatter | solution.py:296
  1148.7 133.0 %reduce-scatter.13.cloned.1.call-done = bf16[2,96,2304]{2,1,0:T(8,128)(2,1)} async-done(((bf16[2,768,2304]{2,1,0:T(8,128)(2,1)}), bf16[2,96,2304]{2,1,0:T(8,128)(2,1)}) %reduce-scatter.13.cloned.1.call-update) | async-done | bytes 884752 | tf_op jit(solution)/shard_map/reduce_scatter | solution.py:290
  1287.3 43.7 %reduce-scatter.23.cloned.1.call-done = bf16[1,768,768]{2,1,0:T(8,128)(2,1)} async-done(((bf16[1,3072,768]{2,1,0:T(8,128)(2,1)}), bf16[1,768,768]{2,1,0:T(8,128)(2,1)}) %reduce-scatter.23.cloned.1.call-update) | async-done | bytes 1179664 | tf_op jit(solution)/shard_map/reduce_scatter | solution.py:281
  1333.8 40.9 %all-reduce = (f32[8]{0:T(128)S(1)}, f32[4,768]{1,0:T(4,128)}, f32[768,8]{0,1:T(8,128)}) all-reduce(f32[8]{0:T(128)S(1)} %broadcast_multiply_fusion.12, f32[4,768]{1,0:T(4,128)S(1)} %pad_maximum_fusion.10, f32[768,8]{0,1:T(8,128)S(1)} %fusion.89), channel_id=1, replica_groups=mesh['dp'=4,'expert'=8] {'dp','expert'}, use_global_device_ids=true, to_apply=%region_35.36 | all-reduce | flops 9224 | bytes 73792 | tf_op jit(solution)/shard_map/psum | solution.py:222
  (345 shorter events, 351.2 us)
Async XLA Ops:
  7.2 296.3 %copy-start = (f32[768,8]{0,1:T(8,128)S(1)}, f32[768,8]{0,1:T(8,128)}, u32[]{:S(2)}) copy-start(f32[768,8]{0,1:T(8,128)} %param.25) | copy-start | bytes 73732
  7.2 59.3 %all-gather.3.cloned.1.call-start = ((), (), s32[]{:S(2)}) async-start(), calls=%async_computation.12 | async-start | bytes 7864320 | tf_op jit(solution)/shard_map/all_gather | solution.py:110
  11.6 137.1 %copy-start.67 = (f32[768]{0:T(1024)}, f32[768]{0:T(1024)S(1)}, u32[]{:S(2)}) copy-start(f32[768]{0:T(1024)S(1)} %get-tuple-element.117) | copy-start | bytes 9220
  11.6 147.4 %copy-start.65 = (f32[768]{0:T(1024)}, f32[768]{0:T(1024)S(1)}, u32[]{:S(2)}) copy-start(f32[768]{0:T(1024)S(1)} %get-tuple-element.119) | copy-start | bytes 9220
  17.3 193.1 %all-gather.5.cloned.1.call-start = ((), (), s32[]{:S(2)}) async-start(), calls=%async_computation.13 | async-start | bytes 7864320 | tf_op jit(solution)/shard_map/all_gather | solution.py:110
  292.2 155.8 %copy-start.2 = (f32[512,768]{1,0:T(8,128)}, f32[512,768]{1,0:T(8,128)S(1)}, u32[]{:S(2)}) copy-start(f32[512,768]{1,0:T(8,128)S(1)} %get-tuple-element.158) | copy-start | bytes 4718596
  292.3 155.8 %copy-start.49 = (f32[512]{0:T(512)}, f32[512]{0:T(512)S(1)}, u32[]{:S(2)}) copy-start(f32[512]{0:T(512)S(1)} %broadcast_multiply_fusion.8) | copy-start | bytes 6148
  292.6 155.4 %copy-start.51 = (f32[512]{0:T(512)}, f32[512]{0:T(512)S(1)}, u32[]{:S(2)}) copy-start(f32[512]{0:T(512)S(1)} %add_rsqrt_fusion) | copy-start | bytes 6148
  296.5 30.6 %all-to-all-start = ((bf16[8,80,768]{2,1,0:T(8,128)(2,1)}), bf16[8,80,768]{2,1,0:T(8,128)(2,1)}, u32[]{:S(2)}, u32[]{:S(2)}) async-start(bf16[8,80,768]{2,1,0:T(8,128)(2,1)} %bitcast.161), calls=%async_computation | async-start | bytes 1966080 | tf_op jit(solution)/shard_map/all_to_all | solution.py:198
  327.1 28.5 %all-to-all-start.2 = ((bf16[8,80,768]{2,1,0:T(8,128)(2,1)}), bf16[8,80,768]{2,1,0:T(8,128)(2,1)}, u32[]{:S(2)}, u32[]{:S(2)}) async-start(bf16[8,80,768]{2,1,0:T(8,128)(2,1)} %bitcast.162), calls=%async_computation.2 | async-start | bytes 1966080 | tf_op jit(solution)/shard_map/all_to_all | solution.py:238
  355.6 28.5 %all-to-all-start.1 = ((bf16[8,80,768]{2,1,0:T(8,128)(2,1)}), bf16[8,80,768]{2,1,0:T(8,128)(2,1)}, u32[]{:S(2)}, u32[]{:S(2)}) async-start(bf16[8,80,768]{2,1,0:T(8,128)(2,1)} %bitcast.176), calls=%async_computation.1 | async-start | bytes 1966080 | tf_op jit(solution)/shard_map/all_to_all | solution.py:211
  384.1 54.0 %all-to-all-start.3 = ((bf16[8,80,768]{2,1,0:T(8,128)(2,1)}), bf16[8,80,768]{2,1,0:T(8,128)(2,1)}, u32[]{:S(2)}, u32[]{:S(2)}) async-start(bf16[8,80,768]{2,1,0:T(8,128)(2,1)} %bitcast.175), calls=%async_computation.3 | async-start | bytes 1966080 | tf_op jit(solution)/shard_map/all_to_all | solution.py:250
  388.3 238.9 %reduce-scatter.9.cloned.1.call-start = ((), (), s32[]{:S(2)}) async-start(), calls=%async_computation.14 | async-start | bytes 7864320 | tf_op jit(solution)/shard_map/reduce_scatter | solution.py:130
  568.6 258.9 %reduce-scatter.11.cloned.1.call-start = ((), (), s32[]{:S(2)}) async-start(), calls=%async_computation.15 | async-start | bytes 7864320 | tf_op jit(solution)/shard_map/reduce_scatter | solution.py:130
  768.9 108.8 %reduce-scatter.21.cloned.1.call-start = ((), (), s32[]{:S(2)}) async-start(), calls=%async_computation.20 | async-start | bytes 5898240 | tf_op jit(solution)/shard_map/reduce_scatter | solution.py:278
  777.5 173.7 %reduce-scatter.15.cloned.1.call-start = ((), (), s32[]{:S(2)}) async-start(), calls=%async_computation.17 | async-start | bytes 2654208 | tf_op jit(solution)/shard_map/reduce_scatter | solution.py:293
  783.9 265.8 %reduce-scatter.19.cloned.1.call-start = ((), (), s32[]{:S(2)}) async-start(), calls=%async_computation.19 | async-start | bytes 5308416 | tf_op jit(solution)/shard_map/reduce_scatter | solution.py:299
  792.8 356.0 %reduce-scatter.17.cloned.1.call-start = ((), (), s32[]{:S(2)}) async-start(), calls=%async_computation.18 | async-start | bytes 5308416 | tf_op jit(solution)/shard_map/reduce_scatter | solution.py:296
  800.6 481.1 %reduce-scatter.13.cloned.1.call-start = ((), (), s32[]{:S(2)}) async-start(), calls=%async_computation.16 | async-start | bytes 7962624 | tf_op jit(solution)/shard_map/reduce_scatter | solution.py:290
  835.3 495.6 %reduce-scatter.23.cloned.1.call-start = ((), (), s32[]{:S(2)}) async-start(), calls=%async_computation.21 | async-start | bytes 5898240 | tf_op jit(solution)/shard_map/reduce_scatter | solution.py:281
  847.5 543.4 %all-reduce.4.cloned.1.call-start = ((), (), s32[]{:S(2)}) async-start(), calls=%async_computation.22 | async-start | bytes 4718592 | tf_op jit(solution)/shard_map/psum | solution.py:304
  848.9 432.8 %copy-start.18 = (bf16[512,768]{1,0:T(8,128)(2,1)S(1)}, bf16[512,768]{1,0:T(8,128)(2,1)}, u32[]{:S(2)}) copy-start(bf16[512,768]{1,0:T(8,128)(2,1)} %param.13) | copy-start | bytes 2359300
  848.9 432.8 %copy-start.32 = (bf16[12,64,512]{2,1,0:T(8,128)(2,1)S(1)}, bf16[12,64,512]{2,1,0:T(8,128)(2,1)}, u32[]{:S(2)}) copy-start(bf16[12,64,512]{2,1,0:T(8,128)(2,1)} %multiply_convert_fusion.6) | copy-start | bytes 2359300
  850.1 431.7 %copy-start.84 = (bf16[512,1536]{0,1:T(8,128)(2,1)S(1)}, bf16[512,1536]{0,1:T(8,128)(2,1)}, u32[]{:S(2)}) copy-start(bf16[512,1536]{0,1:T(8,128)(2,1)} %reduce-scatter.11.cloned.1.call-done) | copy-start | bytes 4718596
  (90 other events, 1433.9 us)
Sparse Core Ops, SparseCore 0:
  17.4 49.0 all-gather.2
  164.0 46.3 all-gather.4
  568.7 58.3 reduce-scatter.8
  769.1 58.3 reduce-scatter.10
  829.9 47.8 reduce-scatter.20
  882.1 69.0 reduce-scatter.14
  955.3 94.3 reduce-scatter.18
  1053.7 94.9 reduce-scatter.16
  1152.8 128.7 reduce-scatter.12
  1284.0 46.8 reduce-scatter.22
  1333.7 57.1 all-reduce.3
where the time goes:
time: 1410 us
  waiting for transfers between devices  655 us (46%)
  matrix products  392 us (28%)
  other arithmetic  175 us (12%)
  blocking collectives  82.3 us (6%)
  local copies, waits for them, and re-layouts  63.3 us (4%)
  starting transfers between devices  19.7 us (1%)
  between operations  18.8 us (1%)
    reduce_scatter x1, waiting for transfers between devices, body(): lax.psum_scatter(qkv_local.astype(jnp.bfloat16), 'expert', scatter_dimens...  133 us
    reduce_scatter x1, waiting for transfers between devices, body(): lax.psum_scatter(up_local.astype(jnp.bfloat16), 'expert', scatter_dimensi...  99.1 us
    reduce_scatter x1, waiting for transfers between devices, body(): lax.psum_scatter(down_local.astype(jnp.bfloat16), 'expert', scatter_dimen...  98.4 us
    all_gather x2, waiting for transfers between devices, attention_forward(): gathered = lax.all_gather(packed[:, model_width:], 'dp', axis=0, tiled=True)  91.1 us
    psum x2, blocking collectives, body(): lax.psum((jnp.sum(one_hot, axis=0), switch * jnp.sum(one_hot * gates[:, N...  82.3 us
    convert_element_type x2, other arithmetic, one_block(): grad_scores = (probs * (grad_probs - inner)).astype(bfloat)  80.7 us
    dot_general x2, matrix products, one_block(): jnp.einsum('qhd,khd->hqk', grad_heads, values, preferred_element_type=sin...  74.4 us
    reduce_scatter x1, waiting for transfers between devices, body(): lax.psum_scatter(out_local.astype(jnp.bfloat16), 'expert', scatter_dimens...  70.4 us
  transfers between devices with their start and end apart: 15, of which 14 were waited for; matrix products, arithmetic and copies ran while one was open for 11% of the time, Pallas kernels for 0%

commit v1 on v0

--- a/solution.py
+++ b/solution.py
@@ -1,6 +1,8 @@
 import jax
 import jax.numpy as jnp
 from jax import lax
+from jax.experimental import pallas as pl
+from jax.experimental.pallas import tpu as pltpu
 from jax.sharding import PartitionSpec as P
 
 H = 12
@@ -102,7 +104,13 @@
     )
 
 
+def two_chips(stream):
+    return lax.axis_size("dp") == 4 and stream.shape[0] % 256 == 0 and stream.shape[1] == H * HD == 768
+
+
 def attention_forward(stream, gain, w_qkv, w_out, offset):
+    if two_chips(stream):
+        return attention_forward_fast(stream, gain, w_qkv, w_out)
     row_count, model_width = stream.shape
     normed_out, normed, factor = norm_forward(stream, gain)
     normed_low = normed_out.astype(bfloat)
@@ -119,6 +127,8 @@
 
 
 def attention_backward(upstream, saved, gain, w_qkv, w_out, offset):
+    if two_chips(upstream):
+        return attention_backward_fast(upstream, saved, gain, w_qkv, w_out)
     normed, factor, normed_low, queries, keys, values, log_sums, mixed = saved
     branch_low = upstream.astype(bfloat)
     out_weight_grad = jnp.dot(mixed.T, branch_low, preferred_element_type=single)
@@ -135,6 +145,477 @@
     normed_grad = jnp.dot(packed_grad, w_qkv.T, preferred_element_type=single)
     stream_grad, gain_grad = norm_backward(normed_grad, normed, factor, gain)
     return (upstream + stream_grad, gain_grad, qkv_weight_grad, out_weight_grad)
+
+
+def mm(left, right, dims=((1,), (0,))):
+    return lax.dot_general(left, right, (dims, ((), ())), preferred_element_type=single)
+
+
+NT = ((1,), (1,))
+MESH = pl.DeviceIdType.MESH
+
+
+def head_lanes(shape, head):
+    return lax.broadcasted_iota(jnp.int32, shape, 1) // HD == head
+
+
+def greet(partners):
+    barrier = pltpu.get_barrier_semaphore()
+    for partner in partners:
+        pl.semaphore_signal(barrier, inc=1, device_id=partner, device_id_type=MESH)
+    pl.semaphore_wait(barrier, len(partners))
+
+
+def send(src, dst, send_sem, recv_sem, target):
+    return pltpu.make_async_remote_copy(
+        src_ref=src,
+        dst_ref=dst,
+        send_sem=send_sem,
+        recv_sem=recv_sem,
+        device_id=target,
+        device_id_type=MESH,
+    )
+
+
+def pair_forward(q_of, keys, values_t, causal, put, half):
+    for j in range(2):
+        key_rows = (j + 1) * half if causal else 2 * half
+        q = q_of(j) * bfloat(HD**-0.5)
+        parts, stats = [], []
+        for head in range(2):
+            own = jnp.where(head_lanes(q.shape, head), q, bfloat(0))
+            scores = mm(keys[:key_rows], own, NT)
+            if causal:
+                place = lax.broadcasted_iota(jnp.int32, (half, half), 0)
+                query = lax.broadcasted_iota(jnp.int32, (half, half), 1)
+                last = jnp.where(place <= query, scores[key_rows - half :], -1e30)
+                if j:
+                    last = jnp.concatenate([scores[: key_rows - half], last], axis=0)
+                scores = last
+            largest = jnp.max(scores, axis=0, keepdims=True)
+            weights = jnp.exp(scores - largest)
+            total = jnp.sum(weights, axis=0, keepdims=True)
+            mixed = mm(values_t[head * HD : (head + 1) * HD, :key_rows], weights.astype(bfloat))
+            parts.append(mixed / total)
+            stats.append(largest + jnp.log(total))
+        put(j, jnp.transpose(jnp.concatenate(parts, axis=0)).astype(bfloat), stats)
+
+
+def forward_kernel(
+    u_ref, gain_ref, wqkv_ref, wout_ref,
+    h_ref, a_ref, o_ref, lse_ref, sv_ref, qx_out_ref,
+    own, sv, qx, ox, od, oc, lsx, lsm, lsd, lsc,
+    core_sem, q_sem, ox_sem, lsx_sem, od_sem, lsd_sem, local_sem,
+):
+    place = lax.axis_index("dp")
+    ex = lax.axis_index("expert")
+    chip = place // 2
+    core = lax.rem(place, 2)
+    other = 1 - core
+    half = u_ref.shape[0]
+    width = u_ref.shape[1]
+    partner = (chip * 2 + other, ex)
+    far = [((1 - chip) * 2 + t, ex) for t in range(2)]
+    greet([partner] + far)
+    stream = u_ref[...]
+    centered = stream - jnp.mean(stream, axis=-1, keepdims=True)
+    factor = lax.rsqrt(jnp.mean(centered * centered, axis=-1, keepdims=True) + eps_norm)
+    a_ref[...] = (centered * factor * gain_ref[...]).astype(bfloat)
+    core_copies = []
+    for i in range(3):
+        part = mm(a_ref[...], wqkv_ref[:, i * width : (i + 1) * width]).astype(bfloat)
+        for p in range(6):
+            own[i, p] = part[:, p * 128 : (p + 1) * 128]
+        copy = send(
+            own.at[i, pl.ds(other * 3, 3)], sv.at[i, :, core], core_sem.at[0, i], core_sem.at[1, i], partner
+        )
+        copy.start()
+        core_copies.append(copy)
+        local = pltpu.make_async_copy(own.at[i, pl.ds(core * 3, 3)], sv.at[i, :, core], local_sem.at[i])
+        local.start()
+        core_copies.append(local)
+        if i == 0:
+
+            @pl.when(chip == 1)
+            def _():
+                for p in range(3):
+                    for s in range(2):
+                        send(
+                            own.at[0, 3 * s + p], qx.at[p, core], q_sem.at[0, p, s], q_sem.at[1, p, core], far[s]
+                        ).start()
+
+    for copy in core_copies:
+        copy.wait()
+    lsm[...] = jnp.zeros_like(lsm)
+    lsx[...] = jnp.zeros_like(lsx)
+
+    def diagonal(p):
+        keys = sv[1, p].reshape(2 * half, 128)
+        values_t = jnp.transpose(sv[2, p].reshape(2 * half, 128).astype(single)).astype(bfloat)
+
+        def put(j, mixed, stats):
+            od[j, p] = mixed
+            for head in range(2):
+                lsm[j, pl.ds(2 * p + head, 1)] = stats[head]
+
+        pair_forward(lambda j: sv[0, p, j], keys, values_t, True, put, half)
+
+    diagonal(0)
+
+    @pl.when(chip == 0)
+    def _():
+        def cross(p, carry):
+            for t in range(2):
+                send(own.at[0, 0], qx.at[p, t], q_sem.at[0, p, t], q_sem.at[1, p, t], partner).wait_recv()
+            keys = sv[1, p].reshape(2 * half, 128)
+            values_t = jnp.transpose(sv[2, p].reshape(2 * half, 128).astype(single)).astype(bfloat)
+
+            def put(j, mixed, stats):
+                ox[p, j] = mixed
+                for head in range(2):
+                    lsx[j, pl.ds(2 * p + head, 1)] = stats[head]
+
+            pair_forward(lambda j: qx[p, j], keys, values_t, False, put, half)
+            for t in range(2):
+                send(ox.at[p, t], oc.at[core * 3 + p], ox_sem.at[0, p, t], ox_sem.at[1, core * 3 + p, 0], far[t]).start()
+            return carry
+
+        lax.fori_loop(0, 3, cross, 0)
+        for t in range(2):
+            send(lsx.at[t], lsc.at[core], lsx_sem.at[0, t], lsx_sem.at[1, core], far[t]).start()
+
+    for p in range(1, 3):
+        diagonal(p)
+    back = [
+        send(od.at[other], oc.at[pl.ds(6 + core * 3, 3)], od_sem.at[0], od_sem.at[1], partner),
+        send(lsm.at[other], lsd, lsd_sem.at[0], lsd_sem.at[1], partner),
+    ]
+    for copy in back:
+        copy.start()
+    sv_ref[...] = sv[...]
+    for copy in back:
+        copy.wait()
+
+    def assemble(s, p):
+        mine = s == core
+        return jnp.where(mine, od[core, p], oc[6 + s * 3 + p])
+
+    @pl.when(chip == 0)
+    def _():
+        for s in range(2):
+            lse_ref[s] = jnp.where(s == core, lsm[core], lsd[...])
+            for p in range(3):
+                o_ref[:, (3 * s + p) * 128 : (3 * s + p + 1) * 128] = assemble(s, p)
+        qx_out_ref[...] = qx[...]
+        for p in range(3):
+            for t in range(2):
+                send(ox.at[p, t], oc.at[p], ox_sem.at[0, p, t], ox_sem.at[1, p, 0], far[t]).wait_send()
+        for t in range(2):
+            send(lsx.at[t], lsc.at[t], lsx_sem.at[0, t], lsx_sem.at[1, t], far[t]).wait_send()
+
+    @pl.when(chip == 1)
+    def _():
+        for p in range(3):
+            for s in range(2):
+                send(own.at[0, 3 * s + p], qx.at[p, s], q_sem.at[0, p, s], q_sem.at[1, p, s], far[s]).wait_send()
+        for s in range(2):
+            send(lsx.at[s], lsc.at[s], lsx_sem.at[0, s], lsx_sem.at[1, s], far[s]).wait_recv()
+            near = jnp.where(s == core, lsm[core], lsd[...])
+            distant = lsc[s]
+            top = jnp.maximum(near, distant)
+            joint = top + jnp.log(jnp.exp(near - top) + jnp.exp(distant - top))
+            lse_ref[s] = joint
+            weights = jnp.concatenate([jnp.exp(near - joint), jnp.exp(distant - joint), jnp.zeros((112, half), single)], axis=0)
+            weights = jnp.transpose(weights)
+            for p in range(3):
+                send(ox.at[p, s], oc.at[3 * s + p], ox_sem.at[0, p, s], ox_sem.at[1, 3 * s + p, 0], far[s]).wait_recv()
+                lanes = head_lanes((half, 128), 0)
+                scale = [jnp.where(lanes, weights[:, r : r + 1], weights[:, r + 1 : r + 2]) for r in (2 * p, 8 + 2 * p)]
+                joined = assemble(s, p).astype(single) * scale[0] + oc[3 * s + p].astype(single) * scale[1]
+                o_ref[:, (3 * s + p) * 128 : (3 * s + p + 1) * 128] = joined.astype(bfloat)
+        qx_out_ref[...] = jnp.zeros_like(qx_out_ref)
+
+    h_ref[...] = u_ref[...] + mm(o_ref[...], wout_ref[...])
+
+
+def kernel_call(kernel, outs, scratch, collective, flops, vmem=56):
+    vmem_spec = pl.BlockSpec(memory_space=pltpu.VMEM)
+    return lambda *args: pl.pallas_call(
+        kernel,
+        out_shape=tuple(jax.ShapeDtypeStruct(*o) for o in outs),
+        in_specs=[vmem_spec] * len(args),
+        out_specs=tuple(vmem_spec for _ in outs),
+        scratch_shapes=scratch,
+        compiler_params=pltpu.CompilerParams(
+            collective_id=collective, has_side_effects=True, vmem_limit_bytes=vmem * 2**20
+        ),
+        cost_estimate=pl.CostEstimate(flops=flops, bytes_accessed=12 * 2**20, transcendentals=0),
+        name=kernel.__name__,
+    )(*args)
+
+
+def attention_forward_fast(stream, gain, w_qkv, w_out):
+    rows, width = stream.shape
+    dma, vm = pltpu.SemaphoreType.DMA, pltpu.VMEM
+    tile = (rows, 128)
+    outs = [
+        ((rows, width), single),
+        ((rows, width), bfloat),
+        ((rows, width), bfloat),
+        ((2, 8, rows), single),
+        ((3, 3, 2) + tile, bfloat),
+        ((3, 2) + tile, bfloat),
+    ]
+    scratch = [
+        vm((3, 6) + tile, bfloat),
+        vm((3, 3, 2) + tile, bfloat),
+        vm((3, 2) + tile, bfloat),
+        vm((3, 2) + tile, bfloat),
+        vm((2, 3) + tile, bfloat),
+        vm((12,) + tile, bfloat),
+        vm((2, 8, rows), single),
+        vm((2, 8, rows), single),
+        vm((8, rows), single),
+        vm((2, 8, rows), single),
+        dma((2, 3)),
+        dma((2, 3, 2)),
+        dma((2, 6, 2)),
+        dma((2, 2)),
+        dma((2,)),
+        dma((2,)),
+        dma((3,)),
+    ]
+    h, a, o, lse, sv, qx = kernel_call(forward_kernel, outs, scratch, 1, 40 * 10**9)(
+        stream, gain.reshape(1, width), w_qkv, w_out
+    )
+    return h, (stream, a, o, lse, sv, qx)
+
+
+def pair_backward(q_of, do_of, stat_of, keys, keys_t, values, causal, put_query, grads, half):
+    key_grad, value_grad, p = grads
+    step = half // 2
+    for j in range(4):
+        key_rows = (j + 1) * step if causal else 2 * half
+        q = q_of(j) * bfloat(HD**-0.5)
+        do = do_of(j)
+        lse, delta = stat_of(j)
+        parts = []
+        for head in range(2):
+            lanes = head_lanes(q.shape, head)
+            own_q = jnp.where(lanes, q, bfloat(0))
+            own_do = jnp.where(lanes, do, bfloat(0))
+            scores = mm(keys[:key_rows], own_q, NT)
+            grad_probs = mm(values[:key_rows], own_do, NT)
+            probs = jnp.exp(scores - lse[head])
+            if causal:
+                place = lax.broadcasted_iota(jnp.int32, (step, step), 0)
+                query = lax.broadcasted_iota(jnp.int32, (step, step), 1)
+                last = jnp.where(place <= query, probs[key_rows - step :], 0.0)
+                if j:
+                    last = jnp.concatenate([probs[: key_rows - step], last], axis=0)
+                probs = last
+            grad_scores = (probs * (grad_probs - delta[head])).astype(bfloat)
+            value_grad[p, :key_rows] += mm(probs.astype(bfloat), own_do)
+            key_grad[p, :key_rows] += mm(grad_scores, own_q)
+            parts.append(mm(keys_t[head * HD : (head + 1) * HD, :key_rows], grad_scores))
+        put_query(j, jnp.transpose(jnp.concatenate(parts, axis=0)) * HD**-0.5)
+
+
+def backward_kernel(
+    dh_ref, u_ref, gain_ref, o_ref, lse_ref, sv, qx, wqkv_ref, wout_ref,
+    du_ref, dgain_ref, dqkv_ref, dbr_ref,
+    do_own, st_own, dob, stb, dox, stx, dk, dv, dqs, dkv_out, dqx, dq_far, landed,
+    core_sem, st_sem, x_sem, stx_sem, dqx_sem, out_sem, local_sem,
+):
+    place = lax.axis_index("dp")
+    ex = lax.axis_index("expert")
+    chip = place // 2
+    core = lax.rem(place, 2)
+    other = 1 - core
+    half, width = u_ref.shape
+    partner = (chip * 2 + other, ex)
+    far = [((1 - chip) * 2 + t, ex) for t in range(2)]
+    greet([partner] + far)
+    dbr_ref[...] = dh_ref[...].astype(bfloat)
+    do = mm(dbr_ref[...], wout_ref[...], NT).astype(bfloat)
+    for p in range(6):
+        do_own[p] = do[:, p * 128 : (p + 1) * 128]
+    row = lax.broadcasted_iota(jnp.int32, (16, width), 0)
+    head_of_row = (row // 8) * 6 + row % 8
+    lane_head = lax.broadcasted_iota(jnp.int32, (16, width), 1) // HD
+    picks = jnp.where(jnp.logical_and(head_of_row == lane_head, row % 8 < 6), 1.0, 0.0)
+    deltas = lax.dot_general(
+        picks,
+        do.astype(single) * o_ref[...].astype(single),
+        (NT, ((), ())),
+        precision=highest,
+        preferred_element_type=single,
+    )
+    for s in range(2):
+        st_own[s, 0:8] = lse_ref[s]
+        st_own[s, 8:16] = deltas[8 * s : 8 * s + 8]
+    first = [
+        send(st_own.at[other], stb.at[core], st_sem.at[0], st_sem.at[1], partner),
+        send(do_own.at[pl.ds(other * 3, 3)], dob.at[:, core], core_sem.at[0], core_sem.at[1], partner),
+        pltpu.make_async_copy(st_own.at[core], stb.at[core], local_sem.at[0]),
+        pltpu.make_async_copy(do_own.at[pl.ds(core * 3, 3)], dob.at[:, core], local_sem.at[1]),
+    ]
+    for copy in first:
+        copy.start()
+
+    @pl.when(chip == 1)
+    def _():
+        for s in range(2):
+            send(st_own.at[s], stx.at[core], stx_sem.at[0, s], stx_sem.at[1, core], far[s]).start()
+        for p in range(3):
+            for s in range(2):
+                send(do_own.at[3 * s + p], dox.at[p, core], x_sem.at[0, p, s], x_sem.at[1, p, core], far[s]).start()
+
+    dk[...] = jnp.zeros_like(dk)
+    dv[...] = jnp.zeros_like(dv)
+    for copy in first:
+        copy.wait()
+
+    def operands(p):
+        keys = sv[1, p].reshape(2 * half, 128)
+        keys_t = jnp.transpose(keys.astype(single)).astype(bfloat)
+        return keys, keys_t, sv[2, p].reshape(2 * half, 128)
+
+    step = half // 2
+
+    def rows_of(j):
+        return pl.ds((j % 2) * step, step)
+
+    def stats_of(ref, p):
+        def at(j):
+            cols = slice((j % 2) * step, (j % 2 + 1) * step)
+            lse = [ref[j // 2, pl.ds(2 * p + head, 1), cols] for head in range(2)]
+            delta = [ref[j // 2, pl.ds(8 + 2 * p + head, 1), cols] for head in range(2)]
+            return lse, delta
+
+        return at
+
+    def diagonal(p):
+        keys, keys_t, values = operands(p)
+
+        def put(j, grad):
+            dqs[p, j // 2, rows_of(j)] = grad.astype(bfloat)
+
+        pair_backward(
+            lambda j: sv[0, p, j // 2, rows_of(j)],
+            lambda j: dob[p, j // 2, rows_of(j)],
+            stats_of(stb, p), keys, keys_t, values, True, put, (dk, dv, p), half,
+        )
+
+    diagonal(0)
+
+    @pl.when(chip == 0)
+    def _():
+        for t in range(2):
+            send(st_own.at[0], stx.at[t], stx_sem.at[0, t], stx_sem.at[1, t], partner).wait_recv()
+
+        def cross(p, carry):
+            for t in range(2):
+                send(do_own.at[0], dox.at[p, t], x_sem.at[0, p, t], x_sem.at[1, p, t], partner).wait_recv()
+            keys, keys_t, values = operands(p)
+
+            def put(j, grad):
+                dqx[p, j // 2, rows_of(j)] = grad.astype(bfloat)
+
+            pair_backward(
+                lambda j: qx[p, j // 2, rows_of(j)],
+                lambda j: dox[p, j // 2, rows_of(j)],
+                stats_of(stx, p), keys, keys_t, values, False, put, (dk, dv, p), half,
+            )
+            for t in range(2):
+                send(dqx.at[p, t], dq_far.at[core * 3 + p], dqx_sem.at[0, p, t], dqx_sem.at[1, core * 3 + p, 0], far[t]).start()
+            return carry
+
+        lax.fori_loop(0, 3, cross, 0)
+
+    for p in range(1, 3):
+        diagonal(p)
+    for p in range(3):
+        for t in range(2):
+            rows = slice(t * half, (t + 1) * half)
+            dkv_out[t, 0, p] = dqs[p, t]
+            dkv_out[t, 1, p] = dk[p, rows].astype(bfloat)
+            dkv_out[t, 2, p] = dv[p, rows].astype(bfloat)
+    last = send(dkv_out.at[other], landed, out_sem.at[0], out_sem.at[1], partner)
+    last.start()
+    last.wait()
+
+    for i in range(3):
+        for s in range(2):
+            for p in range(3):
+                part = jnp.where(s == core, dkv_out[core, i, p], landed[i, p])
+                dqkv_ref[:, i * width + (3 * s + p) * 128 : i * width + (3 * s + p + 1) * 128] = part
+
+    @pl.when(chip == 0)
+    def _():
+        for p in range(3):
+            for t in range(2):
+                send(dqx.at[p, t], dq_far.at[p], dqx_sem.at[0, p, t], dqx_sem.at[1, p, 0], far[t]).wait_send()
+
+    @pl.when(chip == 1)
+    def _():
+        for s in range(2):
+            send(st_own.at[s], stx.at[s], stx_sem.at[0, s], stx_sem.at[1, s], far[s]).wait_send()
+        for p in range(3):
+            for s in range(2):
+                send(do_own.at[3 * s + p], dox.at[p, s], x_sem.at[0, p, s], x_sem.at[1, p, s], far[s]).wait_send()
+        for s in range(2):
+            for p in range(3):
+                q = 3 * s + p
+                send(dqx.at[p, s], dq_far.at[q], dqx_sem.at[0, p, s], dqx_sem.at[1, q, 0], far[s]).wait_recv()
+                cols = slice(q * 128, (q + 1) * 128)
+                dqkv_ref[:, cols] = (dqkv_ref[:, cols].astype(single) + dq_far[q].astype(single)).astype(bfloat)
+
+    da = mm(dqkv_ref[...], wqkv_ref[...], NT)
+    stream = u_ref[...]
+    centered = stream - jnp.mean(stream, axis=-1, keepdims=True)
+    factor = lax.rsqrt(jnp.mean(centered * centered, axis=-1, keepdims=True) + eps_norm)
+    normed = centered * factor
+    dgain_ref[...] = jnp.sum(da * normed, axis=0, keepdims=True)
+    dn = da * gain_ref[...]
+    inner = jnp.mean(dn * normed, axis=-1, keepdims=True)
+    du_ref[...] = dh_ref[...] + factor * (dn - jnp.mean(dn, axis=-1, keepdims=True) - normed * inner)
+
+
+def attention_backward_fast(upstream, saved, gain, w_qkv, w_out):
+    stream, a, o, lse, sv, qx = saved
+    rows, width = stream.shape
+    dma, vm = pltpu.SemaphoreType.DMA, pltpu.VMEM
+    tile = (rows, 128)
+    outs = [((rows, width), single), ((1, width), single), ((rows, 3 * width), bfloat), ((rows, width), bfloat)]
+    scratch = [
+        vm((6,) + tile, bfloat),
+        vm((2, 16, rows), single),
+        vm((3, 2) + tile, bfloat),
+        vm((2, 16, rows), single),
+        vm((3, 2) + tile, bfloat),
+        vm((2, 16, rows), single),
+        vm((3, 2 * rows, 128), single),
+        vm((3, 2 * rows, 128), single),
+        vm((3, 2) + tile, bfloat),
+        vm((2, 3, 3) + tile, bfloat),
+        vm((3, 2) + tile, bfloat),
+        vm((6,) + tile, bfloat),
+        vm((3, 3) + tile, bfloat),
+        dma((2,)),
+        dma((2,)),
+        dma((2, 3, 2)),
+        dma((2, 2)),
+        dma((2, 6, 2)),
+        dma((2,)),
+        dma((2,)),
+    ]
+    du, dgain, dqkv, dbr = kernel_call(backward_kernel, outs, scratch, 2, 60 * 10**9)(
+        upstream, stream, gain.reshape(1, width), o, lse, sv, qx, w_qkv, w_out
+    )
+    out_weight_grad = jnp.dot(o.T, dbr, preferred_element_type=single)
+    qkv_weight_grad = jnp.dot(a.T, dqkv, preferred_element_type=single)
+    return du, dgain[0], qkv_weight_grad, out_weight_grad
 
 
 def routing(expert_ids, expert_count, capacity):

time: 1410 us -> 984 us (0.70)
  matrix products: 392 us -> 109 us
  Pallas kernels: 0 us -> 181 us
  waiting for transfers between devices: 655 us -> 494 us
  other arithmetic: 175 us -> 43.4 us
  local copies, waits for them, and re-layouts: 63.3 us -> 25.9 us
    dot_general x24 -> x4, matrix products: 297 us -> 9.44 us  [the longest x2 5.42 us: attention_backward_fast(): qkv_weight_grad = jnp.dot(a.T, dqkv, preferred_element_type=single)]
    pallas_call x0 -> x4, Pallas kernels: none -> 181 us  [kernel_call(): pl.pallas_call(kernel, out_shape=tuple((jax.ShapeDtypeStruct(*o) for o in...]
    all_gather x2 -> x0, waiting for transfers between devices: 91.1 us -> none  [attention_forward(): gathered = lax.all_gather(packed[:, model_width:], 'dp', axis=0, tiled=True)]
    convert_element_type x2 -> x1, other arithmetic: 80.7 us -> 2.54 us  [body(): inputs = tokens.astype(single)]
    reduce_scatter x2 -> x0, waiting for transfers between devices: 48.3 us -> none  [attention_backward(): lax.psum_scatter(all_grads.astype(jnp.bfloat16), 'dp', scatter_dimension=...]
    reduce_scatter x1, waiting for transfers between devices: 70.4 us -> 23 us  [body(): lax.psum_scatter(out_local.astype(jnp.bfloat16), 'expert', scatter_dimens...]
    psum x1, waiting for transfers between devices: 11.8 us -> 56.2 us  [body(): lax.psum(qkv_part.astype(jnp.bfloat16), 'dp').astype(jnp.float32)]
    reduce_sum x2 -> x0, other arithmetic: 43.9 us -> none  [one_block(): weight_sum = jnp.sum(weights, axis=-1, keepdims=True)]
  transfers between devices with their start and end apart: 15 -> 11, of which waited for: 14 -> 10; matrix products, arithmetic and copies ran while one was open for 11% -> 9% of each run, Pallas kernels for 0% -> 0%
where the time goes in v1:
time: 984 us; the launch traced here: 976 us
  waiting for transfers between devices  494 us (50%)
  Pallas kernels  181 us (18%)
  matrix products  109 us (11%)
  blocking collectives  86.9 us (9%)
  other arithmetic  43.4 us (4%)
  local copies, waits for them, and re-layouts  25.9 us (3%)
  starting transfers between devices  18.2 us (2%)
  between operations  18.2 us (2%)
    pallas_call x4, Pallas kernels, kernel_call(): pl.pallas_call(kernel, out_shape=tuple((jax.ShapeDtypeStruct(*o) for o in...  181 us
    reduce_scatter x1, waiting for transfers between devices, body(): lax.psum_scatter(qkv_local.astype(jnp.bfloat16), 'expert', scatter_dimens...  132 us
    reduce_scatter x1, waiting for transfers between devices, body(): lax.psum_scatter(up_local.astype(jnp.bfloat16), 'expert', scatter_dimensi...  98.7 us
    reduce_scatter x1, waiting for transfers between devices, body(): lax.psum_scatter(down_local.astype(jnp.bfloat16), 'expert', scatter_dimen...  98.1 us
    psum x2, blocking collectives, body(): lax.psum((jnp.sum(one_hot, axis=0), switch * jnp.sum(one_hot * gates[:, N...  86.9 us
    psum x1, waiting for transfers between devices, body(): lax.psum(qkv_part.astype(jnp.bfloat16), 'dp').astype(jnp.float32)  56.2 us
    reduce_scatter x1, waiting for transfers between devices, body(): lax.psum_scatter(down_expert_grad[None].astype(jnp.bfloat16), 'dp', scatt...  47.3 us
    reduce_scatter x1, waiting for transfers between devices, body(): lax.psum_scatter(out_local.astype(jnp.bfloat16), 'expert', scatter_dimens...  23 us
  transfers between devices with their start and end apart: 11, of which 10 were waited for; matrix products, arithmetic and copies ran while one was open for 9% of the time, Pallas kernels for 0%

profile of v1, /device:TPU:0, one launch (start us, length us, event | category | flops | bytes accessed | tf_op | source)
XLA Modules:
  0.0 975.9 jit_solution(2579991383545571183)
XLA Ops:
  21.5 39.9 %forward_kernel.2 = (f32[512,768]{1,0:T(8,128)}, bf16[512,768]{1,0:T(8,128)(2,1)}, bf16[512,768]{1,0:T(8,128)(2,1)}, f32[2,8,512]{2,1,0:T(8,128)}, bf16[3,3,2,51...) custom-call(f32[512,768]{1,0:T(8,128)} %convert_element_type.123.u_ref, f32[1,768]{1,0:T(1,128)} %get-tuple-element.78.gain_ref, ...), custom_call_target="tpu_custom_call" | custom-call | flops 40000000000 | bytes 12582912 | tf_op jit(solution)/shard_map/forward_kernel/pallas_call | solution.py:343
  69.5 9.8 %fusion.81 = (bf16[512,768]{1,0:T(8,128)(2,1)}, f32[512,768]{1,0:T(8,128)}) fusion(f32[512,768]{1,0:T(8,128)S(1)} %copy-done.4, bf16[3072,768]{1,0:T(8,128)(2,1)} %param.22, f32[512,3072]{1,0:T(8,128)S(1)} %fusion.79), kind=kOutput, calls=%fused_computation.136 | convolution fusion | flops 2430861312 | bytes 14942208 | tf_op jit(solution)/shard_map/dot_general | solution.py:666
  79.3 40.2 %forward_kernel.3 = (f32[512,768]{1,0:T(8,128)}, bf16[512,768]{1,0:T(8,128)(2,1)}, bf16[512,768]{1,0:T(8,128)(2,1)}, f32[2,8,512]{2,1,0:T(8,128)}, bf16[3,3,2,51...) custom-call(f32[512,768]{1,0:T(8,128)} %get-tuple-element.82.u_ref, f32[1,768]{1,0:T(1,128)} %get-tuple-element.77.gain_ref, ...), custom_call_target="tpu_custom_call" | custom-call | flops 40000000000 | bytes 12582912 | tf_op jit(solution)/shard_map/forward_kernel/pallas_call | solution.py:343
  138.9 18.0 %all-to-all-done = bf16[8,80,768]{2,1,0:T(8,128)(2,1)S(1)} async-done(((bf16[8,80,768]{2,1,0:T(8,128)(2,1)}), bf16[8,80,768]{2,1,0:T(8,128)(2,1)S(1)}, u32[]{:S(2)}, u32[]{:S(2)}) %all-to-all-start) | async-done | bytes 983072 | tf_op jit(solution)/shard_map/all_to_all | solution.py:679
  169.3 7.9 fusion.31
  177.2 8.2 all-to-all-done.2
  189.1 10.3 %fusion.6 = bf16[640,3072]{1,0:T(8,128)(2,1)S(1)} fusion(f32[640,3072]{1,0:T(8,128)} %copy-done.40, bf16[640,768]{1,0:T(8,128)(2,1)} %bitcast.19, bf16[1,3072,768]{2,1,0:T(8,128)(2,1)} %param.24), kind=kOutput, calls=%fused_computation.14 | convolution fusion | flops 3059220480 | bytes 17498112 | tf_op jit(solution)/shard_map/dot_general | solution.py:727
  201.5 6.6 fusion.28
  218.4 46.3 %psum.56 = f32[8]{0:T(128)S(1)} all-reduce(f32[8]{0:T(128)S(1)} %get-tuple-element.61), channel_id=1, replica_groups=mesh['dp'=4,'expert'=8] {'dp','expert'}, use_global_device_ids=true, to_apply=%region_12.13 | all-reduce | flops 8 | bytes 64 | tf_op jit(solution)/shard_map/psum | solution.py:703
  279.6 50.3 %backward_kernel.2 = (f32[512,768]{1,0:T(8,128)}, f32[1,768]{1,0:T(1,128)}, bf16[512,2304]{1,0:T(8,128)(2,1)}, bf16[512,768]{1,0:T(8,128)(2,1)}) custom-call(f32[512,768]{1,0:T(8,128)} %get-tuple-element.75.dh_ref, f32[512,768]{1,0:T(8,128)} %get-tuple-element.82.u_ref, f32[1,768]{1,0:T(1,128)} %get-tuple-element.77.gain_ref, ...), custom_call_target="tpu_custom_call" | custom-call | flops 60000002048 | bytes 12582912 | tf_op jit(solution)/shard_map/backward_kernel/pallas_call | solution.py:343
  332.0 8.8 fusion.13
  340.8 6.4 multiply_reduce_fusion.1
  349.0 50.1 %backward_kernel.3 = (f32[512,768]{1,0:T(8,128)}, f32[1,768]{1,0:T(1,128)}, bf16[512,2304]{1,0:T(8,128)(2,1)}, bf16[512,768]{1,0:T(8,128)(2,1)}) custom-call(f32[512,768]{1,0:T(8,128)} %multiply_add_fusion.dh_ref, f32[512,768]{1,0:T(8,128)} %convert_element_type.123.u_ref, f32[1,768]{1,0:T(1,128)} %get-tuple-element.78.gain_ref, ...), custom_call_target="tpu_custom_call" | custom-call | flops 60000002048 | bytes 12582912 | tf_op jit(solution)/shard_map/backward_kernel/pallas_call | solution.py:343
  402.9 8.3 convolution_convert_fusion.2
  429.6 7.7 fusion.22
  437.6 10.6 %fusion.23 = bf16[1,3072,768]{2,1,0:T(8,128)(2,1)} fusion(bf16[640,768]{1,0:T(8,128)(2,1)} %bitcast.19, f32[640,3072]{1,0:T(8,128)} %copy-done.40), kind=kOutput, calls=%fused_computation.40 | convolution fusion | flops 3039952896 | bytes 13565952 | tf_op jit(solution)/shard_map/dot_general | solution.py:726
  448.3 23.0 %reduce-scatter.9.cloned.1.call-done = bf16[2,96,768]{2,1,0:T(8,128)(2,1)} async-done(((bf16[2,768,768]{2,1,0:T(8,128)(2,1)}), bf16[2,96,768]{2,1,0:T(8,128)(2,1)}) %reduce-scatter.9.cloned.1.call-update) | async-done | bytes 294928 | tf_op jit(solution)/shard_map/reduce_scatter | solution.py:774
  471.3 98.1 %reduce-scatter.13.cloned.1.call-done = bf16[384,768]{1,0:T(8,128)(2,1)} async-done(((bf16[3072,768]{1,0:T(8,128)(2,1)}), bf16[384,768]{1,0:T(8,128)(2,1)}) %reduce-scatter.13.cloned.1.call-update) | async-done | bytes 589840 | tf_op jit(solution)/shard_map/reduce_scatter | solution.py:780
  569.4 98.7 %reduce-scatter.11.cloned.1.call-done = bf16[96,3072]{1,0:T(8,128)(2,1)} async-done(((bf16[768,3072]{1,0:T(8,128)(2,1)}), bf16[96,3072]{1,0:T(8,128)(2,1)}) %reduce-scatter.11.cloned.1.call-update) | async-done | bytes 589840 | tf_op jit(solution)/shard_map/reduce_scatter | solution.py:777
  668.1 132.3 %reduce-scatter.7.cloned.1.call-done = bf16[2,96,2304]{2,1,0:T(8,128)(2,1)} async-done(((bf16[2,768,2304]{2,1,0:T(8,128)(2,1)}), bf16[2,96,2304]{2,1,0:T(8,128)(2,1)}) %reduce-scatter.7.cloned.1.call-update) | async-done | bytes 884752 | tf_op jit(solution)/shard_map/reduce_scatter | solution.py:771
  801.8 40.6 %all-reduce = (f32[8]{0:T(128)S(1)}, f32[4,768]{1,0:T(4,128)}, f32[768,8]{0,1:T(8,128)}) all-reduce(f32[8]{0:T(128)S(1)} %broadcast_multiply_fusion.6, f32[4,768]{1,0:T(4,128)S(1)} %pad_maximum_fusion.2, f32[768,8]{0,1:T(8,128)S(1)} %fusion.40), channel_id=1, replica_groups=mesh['dp'=4,'expert'=8] {'dp','expert'}, use_global_device_ids=true, to_apply=%region_19.20 | all-reduce | flops 9224 | bytes 73792 | tf_op jit(solution)/shard_map/psum | solution.py:703
  843.6 6.9 reduce-scatter.15.cloned.1.call-done
  853.5 47.3 %reduce-scatter.17.cloned.1.call-done = bf16[1,768,768]{2,1,0:T(8,128)(2,1)} async-done(((bf16[1,3072,768]{2,1,0:T(8,128)(2,1)}), bf16[1,768,768]{2,1,0:T(8,128)(2,1)}) %reduce-scatter.17.cloned.1.call-update) | async-done | bytes 1179664 | tf_op jit(solution)/shard_map/reduce_scatter | solution.py:762
  903.7 56.2 %all-reduce.4.cloned.1.call-done = (bf16[2,96,2304]{2,1,0:T(8,128)(2,1)}, bf16[2,96,768]{2,1,0:T(8,128)(2,1)}, bf16[96,3072]{1,0:T(8,128)(2,1)}, bf16[384,768]{1,0:T(8,128)(2,1)}) async-done(((bf16[2,96,2304]{2,1,0:T(8,128)(2,1)}, bf16[2,96,768]{2,1,0:T(8,128)(2,1)}, bf16[96,3072]{1,0:T(8,128)(2,1)}, bf16[384,768]{1,0:T(8,128)(2,1)}), (bf16[2,96,2304]{2,1,0:T(8,128)(2,1)}, bf16[2,96,768]{2,1,0:T(8,128)(2,1)}, ...) | async-done | bytes 2359312 | tf_op jit(solution)/shard_map/psum | solution.py:785
  (179 shorter events, 125.2 us)
Async XLA Ops:
  8.7 268.9 %copy-start.15 = (f32[768]{0:T(1024)}, f32[768]{0:T(1024)S(1)}, u32[]{:S(2)}) copy-start(f32[768]{0:T(1024)S(1)} %get-tuple-element.80) | copy-start | bytes 9220
  121.2 156.3 %copy-start.19 = (f32[512]{0:T(512)}, f32[512]{0:T(512)S(1)}, u32[]{:S(2)}) copy-start(f32[512]{0:T(512)S(1)} %broadcast_multiply_fusion.4) | copy-start | bytes 6148
  126.8 30.1 %all-to-all-start = ((bf16[8,80,768]{2,1,0:T(8,128)(2,1)}), bf16[8,80,768]{2,1,0:T(8,128)(2,1)S(1)}, u32[]{:S(2)}, u32[]{:S(2)}) async-start(bf16[8,80,768]{2,1,0:T(8,128)(2,1)} %bitcast.10), calls=%async_computation | async-start | bytes 1966080 | tf_op jit(solution)/shard_map/all_to_all | solution.py:679
  156.9 28.5 %all-to-all-start.2 = ((bf16[8,80,768]{2,1,0:T(8,128)(2,1)}), bf16[8,80,768]{2,1,0:T(8,128)(2,1)}, u32[]{:S(2)}, u32[]{:S(2)}) async-start(bf16[8,80,768]{2,1,0:T(8,128)(2,1)} %bitcast.18), calls=%async_computation.2 | async-start | bytes 1966080 | tf_op jit(solution)/shard_map/all_to_all | solution.py:719
  185.4 28.1 %all-to-all-start.1 = ((bf16[8,80,768]{2,1,0:T(8,128)(2,1)}), bf16[8,80,768]{2,1,0:T(8,128)(2,1)S(1)}, u32[]{:S(2)}, u32[]{:S(2)}) async-start(bf16[8,80,768]{2,1,0:T(8,128)(2,1)} %bitcast.83), calls=%async_computation.1 | async-start | bytes 1966080 | tf_op jit(solution)/shard_map/all_to_all | solution.py:692
  213.5 55.3 %all-to-all-start.3 = ((bf16[8,80,768]{2,1,0:T(8,128)(2,1)}), bf16[8,80,768]{2,1,0:T(8,128)(2,1)}, u32[]{:S(2)}, u32[]{:S(2)}) async-start(bf16[8,80,768]{2,1,0:T(8,128)(2,1)} %bitcast.82), calls=%async_computation.3 | async-start | bytes 1966080 | tf_op jit(solution)/shard_map/all_to_all | solution.py:731
  217.7 253.6 %reduce-scatter.9.cloned.1.call-start = ((), (), s32[]{:S(2)}) async-start(), calls=%async_computation.11 | async-start | bytes 2654208 | tf_op jit(solution)/shard_map/reduce_scatter | solution.py:774
  402.7 166.7 %reduce-scatter.13.cloned.1.call-start = ((), (), s32[]{:S(2)}) async-start(), calls=%async_computation.13 | async-start | bytes 5308416 | tf_op jit(solution)/shard_map/reduce_scatter | solution.py:780
  411.3 256.8 %reduce-scatter.11.cloned.1.call-start = ((), (), s32[]{:S(2)}) async-start(), calls=%async_computation.12 | async-start | bytes 5308416 | tf_op jit(solution)/shard_map/reduce_scatter | solution.py:777
  417.8 382.6 %reduce-scatter.7.cloned.1.call-start = ((), (), s32[]{:S(2)}) async-start(), calls=%async_computation.10 | async-start | bytes 7962624 | tf_op jit(solution)/shard_map/reduce_scatter | solution.py:771
  428.5 422.1 %reduce-scatter.15.cloned.1.call-start = ((), (), s32[]{:S(2)}) async-start(), calls=%async_computation.14 | async-start | bytes 5898240 | tf_op jit(solution)/shard_map/reduce_scatter | solution.py:759
  437.3 463.5 %reduce-scatter.17.cloned.1.call-start = ((), (), s32[]{:S(2)}) async-start(), calls=%async_computation.15 | async-start | bytes 5898240 | tf_op jit(solution)/shard_map/reduce_scatter | solution.py:762
  448.1 352.3 %copy-start.34 = (f32[8]{0:T(128)S(1)}, f32[8]{0:T(128)}, u32[]{:S(2)}) copy-start(f32[8]{0:T(128)} %get-tuple-element.60) | copy-start | bytes 100
  448.1 352.3 %copy-start.31 = (f32[768]{0:T(1024)S(1)}, f32[768]{0:T(1024)}, u32[]{:S(2)}) copy-start(f32[768]{0:T(1024)} %get-tuple-element.54) | copy-start | bytes 9220
  448.1 352.4 %copy-start.3 = (f32[512,768]{1,0:T(8,128)S(1)}, f32[512,768]{1,0:T(8,128)}, u32[]{:S(2)}) copy-start(f32[512,768]{1,0:T(8,128)} %get-tuple-element.33) | copy-start | bytes 4718596
  448.1 352.4 %copy-start.16 = (f32[768]{0:T(1024)S(1)}, f32[768]{0:T(1024)}, u32[]{:S(2)}) copy-start(f32[768]{0:T(1024)} %copy-done.15) | copy-start | bytes 9220
  448.2 352.4 %copy-start.18 = (s32[512,1]{0,1:T(1,128)S(1)}, s32[512,1]{0,1:T(1,128)}, u32[]{:S(2)}) copy-start(s32[512,1]{0,1:T(1,128)} %param.15) | copy-start | bytes 6148
  448.2 352.4 %copy-start.20 = (f32[512]{0:T(512)S(1)}, f32[512]{0:T(512)}, u32[]{:S(2)}) copy-start(f32[512]{0:T(512)} %copy-done.19) | copy-start | bytes 6148
  448.2 352.4 %copy-start.22 = (f32[512]{0:T(512)S(1)}, f32[512]{0:T(512)}, u32[]{:S(2)}) copy-start(f32[512]{0:T(512)} %copy-done.21) | copy-start | bytes 6148
  448.2 352.4 %copy-start.28 = (f32[512]{0:T(512)S(1)}, f32[512]{0:T(512)}, u32[]{:S(2)}) copy-start(f32[512]{0:T(512)} %copy-done.27) | copy-start | bytes 6148
  448.2 353.5 %copy-start.32 = (f32[1,768]{1,0:T(1,128)S(1)}, f32[1,768]{1,0:T(1,128)}, u32[]{:S(2)}) copy-start(f32[1,768]{1,0:T(1,128)} %get-tuple-element.45) | copy-start | bytes 9220
  448.2 353.5 %copy-start.33 = (f32[1,768]{1,0:T(1,128)S(1)}, f32[1,768]{1,0:T(1,128)}, u32[]{:S(2)}) copy-start(f32[1,768]{1,0:T(1,128)} %get-tuple-element.44) | copy-start | bytes 9220
  448.2 394.1 %copy-start.38 = (f32[8]{0:T(128)S(1)}, f32[8]{0:T(128)}, u32[]{:S(2)}) copy-start(f32[8]{0:T(128)} %copy-done.37) | copy-start | bytes 100
  448.3 511.6 %all-reduce.4.cloned.1.call-start = ((), (), s32[]{:S(2)}) async-start(), calls=%async_computation.16 | async-start | bytes 4718592 | tf_op jit(solution)/shard_map/psum | solution.py:785
  (35 other events, 670.4 us)
Sparse Core Ops, SparseCore 0:
  402.8 68.4 reduce-scatter.8
  475.0 94.4 reduce-scatter.12
  573.1 94.9 reduce-scatter.10
  671.7 128.6 reduce-scatter.6
  803.0 47.5 reduce-scatter.14
  853.0 47.8 reduce-scatter.16
  903.6 56.2 all-reduce.3

commit v2 on v1

--- a/solution.py
+++ b/solution.py
@@ -1,3 +1,5 @@
+import functools
+
 import jax
 import jax.numpy as jnp
 from jax import lax
@@ -104,13 +106,7 @@
     )
 
 
-def two_chips(stream):
-    return lax.axis_size("dp") == 4 and stream.shape[0] % 256 == 0 and stream.shape[1] == H * HD == 768
-
-
 def attention_forward(stream, gain, w_qkv, w_out, offset):
-    if two_chips(stream):
-        return attention_forward_fast(stream, gain, w_qkv, w_out)
     row_count, model_width = stream.shape
     normed_out, normed, factor = norm_forward(stream, gain)
     normed_low = normed_out.astype(bfloat)
@@ -127,8 +123,6 @@
 
 
 def attention_backward(upstream, saved, gain, w_qkv, w_out, offset):
-    if two_chips(upstream):
-        return attention_backward_fast(upstream, saved, gain, w_qkv, w_out)
     normed, factor, normed_low, queries, keys, values, log_sums, mixed = saved
     branch_low = upstream.astype(bfloat)
     out_weight_grad = jnp.dot(mixed.T, branch_low, preferred_element_type=single)
@@ -202,10 +196,10 @@
 
 
 def forward_kernel(
-    u_ref, gain_ref, wqkv_ref, wout_ref,
-    h_ref, a_ref, o_ref, lse_ref, sv_ref, qx_out_ref,
+    index, u_ref, gain_ref, wqkv_any, wout_any, count_ref,
+    h_ref, a_ref, o_ref, lse_ref, sv_ref, qx_out_ref, counts_ref,
     own, sv, qx, ox, od, oc, lsx, lsm, lsd, lsc,
-    core_sem, q_sem, ox_sem, lsx_sem, od_sem, lsd_sem, local_sem,
+    core_sem, q_sem, ox_sem, lsx_sem, od_sem, lsd_sem, local_sem, wqkv_ref, wout_ref, w_sem, counts_in, count_sem,
 ):
     place = lax.axis_index("dp")
     ex = lax.axis_index("expert")
@@ -216,13 +210,29 @@
     width = u_ref.shape[1]
     partner = (chip * 2 + other, ex)
     far = [((1 - chip) * 2 + t, ex) for t in range(2)]
+    loads = [
+        pltpu.make_async_copy(
+            wqkv_any.at[index, :, pl.ds(i * width, width)], wqkv_ref.at[:, pl.ds(i * width, width)], w_sem.at[i]
+        )
+        for i in range(3)
+    ]
+    loads.append(pltpu.make_async_copy(wout_any.at[index], wout_ref, w_sem.at[3]))
+    for load in loads:
+        load.start()
     greet([partner] + far)
+    count_copies = [
+        send(count_ref, counts_in.at[i], count_sem.at[0, i], count_sem.at[1, i], to)
+        for i, to in enumerate([partner, (lax.rem(place + 2, 4), ex), (3 - place, ex)])
+    ]
+    for copy in count_copies:
+        copy.start()
     stream = u_ref[...]
     centered = stream - jnp.mean(stream, axis=-1, keepdims=True)
     factor = lax.rsqrt(jnp.mean(centered * centered, axis=-1, keepdims=True) + eps_norm)
-    a_ref[...] = (centered * factor * gain_ref[...]).astype(bfloat)
+    a_ref[...] = (centered * factor * gain_ref[2 * index : 2 * index + 1]).astype(bfloat)
     core_copies = []
     for i in range(3):
+        loads[i].wait()
         part = mm(a_ref[...], wqkv_ref[:, i * width : (i + 1) * width]).astype(bfloat)
         for p in range(6):
             own[i, p] = part[:, p * 128 : (p + 1) * 128]
@@ -335,26 +345,36 @@
                 o_ref[:, (3 * s + p) * 128 : (3 * s + p + 1) * 128] = joined.astype(bfloat)
         qx_out_ref[...] = jnp.zeros_like(qx_out_ref)
 
+    loads[3].wait()
+    for copy in count_copies:
+        copy.wait()
+    counts_ref[...] = count_ref[...] + counts_in[0] + counts_in[1] + counts_in[2]
     h_ref[...] = u_ref[...] + mm(o_ref[...], wout_ref[...])
 
 
-def kernel_call(kernel, outs, scratch, collective, flops, vmem=56):
+names = (
+    "forward_zero", "forward_one", "backward_zero", "backward_one", "attention_weights_one", "attention_weights_two",
+    "ffn_up_weights", "ffn_down_weights", "experts",
+)
+
+
+def kernel_call(kernel, outs, scratch, name, flops, stay=(), vmem=56):
     vmem_spec = pl.BlockSpec(memory_space=pltpu.VMEM)
     return lambda *args: pl.pallas_call(
         kernel,
         out_shape=tuple(jax.ShapeDtypeStruct(*o) for o in outs),
-        in_specs=[vmem_spec] * len(args),
+        in_specs=[pl.BlockSpec(memory_space=pl.ANY) if i in stay else vmem_spec for i in range(len(args))],
         out_specs=tuple(vmem_spec for _ in outs),
         scratch_shapes=scratch,
         compiler_params=pltpu.CompilerParams(
-            collective_id=collective, has_side_effects=True, vmem_limit_bytes=vmem * 2**20
+            collective_id=1 + names.index(name), has_side_effects=True, vmem_limit_bytes=vmem * 2**20
         ),
         cost_estimate=pl.CostEstimate(flops=flops, bytes_accessed=12 * 2**20, transcendentals=0),
-        name=kernel.__name__,
+        name=name,
     )(*args)
 
 
-def attention_forward_fast(stream, gain, w_qkv, w_out):
+def attention_forward_fast(stream, gains, w_qkv, w_out, counts, index):
     rows, width = stream.shape
     dma, vm = pltpu.SemaphoreType.DMA, pltpu.VMEM
     tile = (rows, 128)
@@ -365,6 +385,7 @@
         ((2, 8, rows), single),
         ((3, 3, 2) + tile, bfloat),
         ((3, 2) + tile, bfloat),
+        ((8, 128), single),
     ]
     scratch = [
         vm((3, 6) + tile, bfloat),
@@ -384,11 +405,21 @@
         dma((2,)),
         dma((2,)),
         dma((3,)),
+        vm(w_qkv.shape[1:], bfloat),
+        vm(w_out.shape[1:], bfloat),
+        dma((4,)),
+        vm((3, 8, 128), single),
+        dma((2, 3)),
     ]
-    h, a, o, lse, sv, qx = kernel_call(forward_kernel, outs, scratch, 1, 40 * 10**9)(
-        stream, gain.reshape(1, width), w_qkv, w_out
-    )
-    return h, (stream, a, o, lse, sv, qx)
+    h, a, o, lse, sv, qx, counts = kernel_call(
+        functools.partial(forward_kernel, index),
+        outs,
+        scratch,
+        ("forward_zero", "forward_one")[index],
+        40 * 10**9,
+        (2, 3),
+    )(stream, gains, w_qkv, w_out, counts)
+    return h, (stream, a, o, lse, sv, qx), counts
 
 
 def pair_backward(q_of, do_of, stat_of, keys, keys_t, values, causal, put_query, grads, half):
@@ -422,10 +453,10 @@
 
 
 def backward_kernel(
-    dh_ref, u_ref, gain_ref, o_ref, lse_ref, sv, qx, wqkv_ref, wout_ref,
+    index, dh_ref, u_ref, gain_ref, o_ref, lse_ref, sv, qx, wqkv_any, wout_any,
     du_ref, dgain_ref, dqkv_ref, dbr_ref,
     do_own, st_own, dob, stb, dox, stx, dk, dv, dqs, dkv_out, dqx, dq_far, landed,
-    core_sem, st_sem, x_sem, stx_sem, dqx_sem, out_sem, local_sem,
+    core_sem, st_sem, x_sem, stx_sem, dqx_sem, out_sem, local_sem, wqkv_ref, wout_ref, w_sem,
 ):
     place = lax.axis_index("dp")
     ex = lax.axis_index("expert")
@@ -435,8 +466,15 @@
     half, width = u_ref.shape
     partner = (chip * 2 + other, ex)
     far = [((1 - chip) * 2 + t, ex) for t in range(2)]
+    loads = [
+        pltpu.make_async_copy(wout_any.at[index], wout_ref, w_sem.at[0]),
+        pltpu.make_async_copy(wqkv_any.at[index], wqkv_ref, w_sem.at[1]),
+    ]
+    for load in loads:
+        load.start()
     greet([partner] + far)
     dbr_ref[...] = dh_ref[...].astype(bfloat)
+    loads[0].wait()
     do = mm(dbr_ref[...], wout_ref[...], NT).astype(bfloat)
     for p in range(6):
         do_own[p] = do[:, p * 128 : (p + 1) * 128]
@@ -571,18 +609,19 @@
                 cols = slice(q * 128, (q + 1) * 128)
                 dqkv_ref[:, cols] = (dqkv_ref[:, cols].astype(single) + dq_far[q].astype(single)).astype(bfloat)
 
+    loads[1].wait()
     da = mm(dqkv_ref[...], wqkv_ref[...], NT)
     stream = u_ref[...]
     centered = stream - jnp.mean(stream, axis=-1, keepdims=True)
     factor = lax.rsqrt(jnp.mean(centered * centered, axis=-1, keepdims=True) + eps_norm)
     normed = centered * factor
     dgain_ref[...] = jnp.sum(da * normed, axis=0, keepdims=True)
-    dn = da * gain_ref[...]
+    dn = da * gain_ref[2 * index : 2 * index + 1]
     inner = jnp.mean(dn * normed, axis=-1, keepdims=True)
     du_ref[...] = dh_ref[...] + factor * (dn - jnp.mean(dn, axis=-1, keepdims=True) - normed * inner)
 
 
-def attention_backward_fast(upstream, saved, gain, w_qkv, w_out):
+def attention_backward_fast(upstream, saved, gains, w_qkv, w_out, index):
     stream, a, o, lse, sv, qx = saved
     rows, width = stream.shape
     dma, vm = pltpu.SemaphoreType.DMA, pltpu.VMEM
@@ -609,13 +648,297 @@
         dma((2, 6, 2)),
         dma((2,)),
         dma((2,)),
+        vm(w_qkv.shape[1:], bfloat),
+        vm(w_out.shape[1:], bfloat),
+        dma((2,)),
     ]
-    du, dgain, dqkv, dbr = kernel_call(backward_kernel, outs, scratch, 2, 60 * 10**9)(
-        upstream, stream, gain.reshape(1, width), o, lse, sv, qx, w_qkv, w_out
-    )
-    out_weight_grad = jnp.dot(o.T, dbr, preferred_element_type=single)
-    qkv_weight_grad = jnp.dot(a.T, dqkv, preferred_element_type=single)
-    return du, dgain[0], qkv_weight_grad, out_weight_grad
+    du, dgain, dqkv, dbr = kernel_call(
+        functools.partial(backward_kernel, index),
+        outs,
+        scratch,
+        ("backward_zero", "backward_one")[index],
+        60 * 10**9,
+        (7, 8),
+    )(upstream, stream, gains, o, lse, sv, qx, w_qkv, w_out)
+    return du, dgain[0], dqkv, dbr
+
+
+def flip_bits(place, bits, count):
+    total = 0
+    for i in range(count):
+        bit = lax.rem(place // 2**i, 2)
+        total = total + 2**i * (1 - bit if bits >> i & 1 else bit)
+    return total
+
+
+def core_sums(product, parts, landed, sems, partner, core, stay_ref, go_ref, axis):
+    left, rights, shards, dense = product
+    groups, unit = parts.shape[1], parts.shape[2]
+    other = 1 - core
+    block = 768
+    deep = left.shape[1]
+    per = deep // shards
+    flipped = [jnp.transpose(left[:, first : first + block]) for first in range(0, deep, block)]
+    pieces = []
+    column = 0
+    for right in rights:
+        wide = right.shape[1]
+        step = 768 if deep == block else 256
+        pieces += [(right, start, column + start, step) for start in range(0, wide, step)]
+        column += wide
+
+    def finish(i):
+        copies[i].wait()
+        _, _, at, step = pieces[i]
+        columns = slice(at, at + step)
+        for g in range(groups // 2):
+            for ref, pick in ((stay_ref, axis), (go_ref, 1 - axis)):
+                spot = 2 * g + pick
+                mine = parts[core, spot, :, columns].astype(single)
+                ref[g, :, columns] = (mine + landed[spot, :, columns].astype(single)).astype(bfloat)
+
+    copies = []
+    for i, (right, start, at, step) in enumerate(pieces):
+        for b, rows in enumerate(flipped):
+            part = mm(rows, right[:, start : start + step]).astype(bfloat)
+            for row in range(0, block, unit):
+                shard, inside = (b * block + row) // per, (b * block + row) % per
+                spot = (inside // unit, shard) if dense else (shard % 2, shard // 2)
+                parts[spot[0], spot[1], :, at : at + step] = part[row : row + unit]
+        columns = pl.ds(at, step)
+        copy = send(parts.at[other, :, :, columns], landed.at[:, :, columns], sems.at[0, i], sems.at[1, i], partner)
+        copy.start()
+        copies.append(copy)
+        if i >= 2:
+            finish(i - 2)
+    for i in range(max(0, len(pieces) - 2), len(pieces)):
+        finish(i)
+
+
+def weight_kernel(products, *refs):
+    count = len(products)
+    scratch = refs[-3 * count :]
+    results = refs[-5 * count : -3 * count]
+    place = lax.axis_index("dp")
+    ex = lax.axis_index("expert")
+    core = lax.rem(place, 2)
+    partner = (place + 1 - 2 * core, ex)
+    greet([partner])
+    for i, (left, rights) in enumerate(products):
+        parts, landed, sems = scratch[3 * i : 3 * i + 3]
+        product = (refs[left], [refs[r] for r in rights], 8, True)
+        core_sums(product, parts, landed, sems, partner, core, *results[2 * i : 2 * i + 2], lax.rem(ex, 2))
+
+
+def sum_scratch(groups, unit, columns):
+    return [
+        pltpu.VMEM((2, groups, unit, columns), bfloat),
+        pltpu.VMEM((groups, unit, columns), bfloat),
+        pltpu.SemaphoreType.DMA((2, 4)),
+    ]
+
+
+def weight_products(products, sources, name):
+    outs, scratch, flops = [], [], 0
+    for left, rights in products:
+        rows, deep = sources[left].shape
+        columns = sum(sources[r].shape[1] for r in rights)
+        outs += [((4, deep // 16, columns), bfloat)] * 2
+        scratch += sum_scratch(8, deep // 16, columns)
+        flops += 4 * rows * deep * columns
+    return kernel_call(functools.partial(weight_kernel, products), outs, scratch, name, flops)(*sources)
+
+
+def expert_kernel(
+    rows_ref, row_target_ref, target_ref, scale_ref, count_ref, upstream_ref, up_any, down_any,
+    result_ref, grad_ref, counts_ref, up_stay, up_go, down_stay, down_go,
+    outgoing, scalars, arrived, scalars_in, acts, dhidden, dresult, back, back_in,
+    up_parts, up_landed, up_sems, down_parts, down_landed, down_sems,
+    up_ref, down_ref, load_sems, out_sems, scalar_sems, back_sems,
+):
+    place = lax.axis_index("dp")
+    ex = lax.axis_index("expert")
+    chip = place // 2
+    core = lax.rem(place, 2)
+    partner = (place + 1 - 2 * core, ex)
+    experts, cap, width = arrived.shape
+    loads = [
+        pltpu.make_async_copy(up_any.at[0], up_ref, load_sems.at[0]),
+        pltpu.make_async_copy(down_any.at[0], down_ref, load_sems.at[1]),
+    ]
+    for load in loads:
+        load.start()
+    far_first = (4, 5, 6, 7, 2, 3, 1)
+    mates = {k: flip_bits(ex, k, 3) for k in far_first}
+    greet([(place, mates[k]) for k in far_first] + [partner])
+    tokens = rows_ref.shape[0]
+    slots = experts * cap
+    slot = lax.broadcasted_iota(jnp.int32, (slots, tokens), 0)
+    picks = jnp.where(slot == row_target_ref[...], 1.0, 0.0).astype(bfloat)
+    sent = mm(picks, rows_ref[...]).astype(bfloat)
+    lane = lax.broadcasted_iota(jnp.int32, (tokens, 128), 1)
+    for e in range(experts):
+        outgoing[e] = sent[e * cap : (e + 1) * cap]
+        here = jnp.logical_and(target_ref[...] == lane + e * cap, lane < cap)
+        line = jnp.sum(jnp.where(here, scale_ref[...], 0.0), axis=0, keepdims=True)
+        scalars[e] = jnp.concatenate([jnp.broadcast_to(line, (4, 128)), count_ref[0:4]], axis=0)
+    for k in far_first:
+        e = mates[k]
+        send(scalars.at[e], scalars_in.at[ex], scalar_sems.at[0, k], scalar_sems.at[1, k], (place, e)).start()
+        send(outgoing.at[e], arrived.at[ex], out_sems.at[0, k], out_sems.at[1, k], (place, e)).start()
+    arrived[ex] = outgoing[ex]
+    scalars_in[ex] = scalars[ex]
+    for load in loads:
+        load.wait()
+    for i in range(4):
+        for k in (2 * i, 2 * i + 1):
+            if k:
+                e = mates[k]
+                send(scalars.at[e], scalars_in.at[e], scalar_sems.at[0, k], scalar_sems.at[1, k], (place, e)).wait()
+                send(outgoing.at[e], arrived.at[e], out_sems.at[0, k], out_sems.at[1, k], (place, e)).wait()
+        j = flip_bits(ex // 2, i, 2)
+        rows = arrived[pl.ds(2 * j, 2)].reshape(2 * cap, width)
+        for b in range(2):
+            column = jnp.transpose(jnp.concatenate([scalars_in[2 * j + b]] * 16, axis=0))[:cap, 0:1]
+            dresult[2 * j + b] = (upstream_ref[2 * j + b].astype(single) * column).astype(bfloat)
+        upstream = dresult[pl.ds(2 * j, 2)].reshape(2 * cap, width)
+        hidden_width = up_ref.shape[1]
+        step = 768
+        total = jnp.zeros((2 * cap, width), single)
+        total_grad = jnp.zeros((2 * cap, width), single)
+        for start in range(0, hidden_width, step):
+            cols = slice(start, start + step)
+            hidden = mm(rows, up_ref[:, cols])
+            grad = mm(upstream, down_ref[cols, :], NT)
+            square = hidden * hidden
+            tanh = jnp.tanh(0.7978845608028654 * hidden * (1.0 + 0.044715 * square))
+            act = (0.5 * hidden * (1.0 + tanh)).astype(bfloat)
+            slope = 0.5 * (1.0 + tanh) + 0.5 * hidden * (1.0 - tanh * tanh) * (
+                0.7978845608028654 * (1.0 + 3 * 0.044715 * square)
+            )
+            dhid = (grad * slope).astype(bfloat)
+            acts[j, :, cols] = act
+            dhidden[j, :, cols] = dhid
+            total = total + mm(act, down_ref[cols, :])
+            total_grad = total_grad + mm(dhid, up_ref[:, cols], NT)
+        for b in range(2):
+            back[0, 2 * j + b] = total_grad[b * cap : (b + 1) * cap].astype(bfloat)
+            back[1, 2 * j + b] = total[b * cap : (b + 1) * cap].astype(bfloat)
+        for k in (2 * i, 2 * i + 1):
+            if k:
+                e = mates[k]
+                send(back.at[0, e], back_in.at[0, ex], back_sems.at[0, 0, k], back_sems.at[0, 1, k], (place, e)).start()
+    for k in far_first:
+        e = mates[k]
+        send(back.at[1, e], back_in.at[1, ex], back_sems.at[1, 0, k], back_sems.at[1, 1, k], (place, e)).start()
+    for half in range(2):
+        back_in[half, ex] = back[half, ex]
+    counts = scalars_in[0]
+    for e in range(1, experts):
+        counts = counts + scalars_in[e]
+    counts_ref[...] = counts
+    core_sums(
+        (arrived.reshape(slots, width), [dhidden.reshape(slots, hidden_width)], 4, False),
+        up_parts, up_landed, up_sems, partner, core, up_stay, up_go, chip,
+    )
+    core_sums(
+        (acts.reshape(slots, hidden_width), [dresult.reshape(slots, width)], 4, False),
+        down_parts, down_landed, down_sems, partner, core, down_stay, down_go, chip,
+    )
+    slot_lane = lax.broadcasted_iota(jnp.int32, (tokens, slots), 1)
+    takes = jnp.where(target_ref[...] == slot_lane, 1.0, 0.0).astype(bfloat)
+    for half, ref in ((0, grad_ref), (1, result_ref)):
+        for k in far_first:
+            e = mates[k]
+            send(
+                back.at[half, e], back_in.at[half, e], back_sems.at[half, 0, k], back_sems.at[half, 1, k], (place, e)
+            ).wait()
+        ref[...] = mm(takes, back_in[half].reshape(slots, width)).astype(bfloat)
+
+
+def expert_layer(rows, target, scale, counts, upstream, w_up, w_down):
+    tokens, width = rows.shape
+    experts, cap = upstream.shape[:2]
+    hidden = w_up.shape[2]
+    dma, vm = pltpu.SemaphoreType.DMA, pltpu.VMEM
+    block = (experts, cap, width)
+    quarter = width // 4
+    outs = [
+        ((tokens, width), bfloat),
+        ((tokens, width), bfloat),
+        ((8, 128), single),
+        ((1, quarter, hidden), bfloat),
+        ((1, quarter, hidden), bfloat),
+        ((1, hidden // 4, width), bfloat),
+        ((1, hidden // 4, width), bfloat),
+    ]
+    scratch = [
+        vm(block, bfloat),
+        vm((experts, 8, 128), single),
+        vm(block, bfloat),
+        vm((experts, 8, 128), single),
+        vm((4, 2 * cap, hidden), bfloat),
+        vm((4, 2 * cap, hidden), bfloat),
+        vm(block, bfloat),
+        vm((2,) + block, bfloat),
+        vm((2,) + block, bfloat),
+        *sum_scratch(2, quarter, hidden),
+        *sum_scratch(2, hidden // 4, width),
+        vm(w_up.shape[1:], bfloat),
+        vm(w_down.shape[1:], bfloat),
+        dma((2,)),
+        dma((2, 8)),
+        dma((2, 8)),
+        dma((2, 2, 8)),
+    ]
+    return kernel_call(expert_kernel, outs, scratch, "experts", 60 * 10**9, (6, 7), 60)(
+        rows, target.reshape(1, tokens), target.reshape(tokens, 1), scale, counts, upstream, w_up, w_down
+    )
+
+
+def swap(array, axis_bit):
+    expert = lax.axis_size("expert")
+    total = lax.axis_size("dp") * expert
+    step = expert << axis_bit if axis_bit < 2 else 1 << (axis_bit - 2)
+    return lax.ppermute(array, ("dp", "expert"), [(i, i ^ step) for i in range(total)])
+
+
+def added(left, right):
+    return (left.astype(single) + right.astype(single)).astype(bfloat)
+
+
+def pick(array, index, axis):
+    return lax.dynamic_index_in_dim(array, index, axis, keepdims=False)
+
+
+def sum_y(stay, go):
+    return added(stay, swap(go, 2))
+
+
+def sum_z(kept):
+    z = lax.axis_index("expert") // 2
+    kept = kept.reshape((2, 2) + kept.shape[1:])
+    kept = added(pick(kept, z % 2, 1), swap(pick(kept, 1 - z % 2, 1), 3))
+    return added(pick(kept, z // 2, 0), swap(pick(kept, 1 - z // 2, 0), 4))
+
+
+def sum_x(kept):
+    kept = added(kept, swap(kept, 1))
+    mate = swap(kept, 0)
+    core = lax.axis_index("dp") % 2
+    first = jnp.where(core == 0, kept, mate).astype(single)
+    second = jnp.where(core == 0, mate, kept).astype(single)
+    return jnp.concatenate([first, second], axis=0)
+
+
+def reduce_small(values):
+    for bit in range(5):
+        values = values + swap(values, bit)
+    return values
+
+
+def after(values, others):
+    return lax.optimization_barrier((values, others))
 
 
 def routing(expert_ids, expert_count, capacity):
@@ -630,7 +953,7 @@
     return (one_hot.astype(single), target, kept_rows)
 
 
-def body(
+def body_any(
     tokens,
     cotangent,
     expert_ids,
@@ -803,6 +1126,133 @@
     )
 
 
+def body_fast(
+    tokens,
+    cotangent,
+    expert_ids,
+    loss_weights,
+    section,
+    norm_gains,
+    attn_qkv,
+    attn_out,
+    ffn_up,
+    ffn_down,
+    expert_up,
+    expert_down,
+    router,
+):
+    row_count, model_width = tokens.shape
+    expert_count = router.shape[1]
+    capacity = 5 * row_count // (4 * expert_count)
+    slots_all = expert_count * capacity
+    group_count = lax.axis_size("expert")
+    total_tokens = row_count * lax.axis_size("dp") * group_count
+    sequence = lax.axis_index("expert")
+    switch = section[sequence].astype(single)
+    seq_weight = loss_weights[sequence].astype(single)
+    one_hot, target, kept_rows = routing(expert_ids, expert_count, capacity)
+    count_tile = jnp.zeros((8, 128), single).at[:, :expert_count].set(jnp.sum(one_hot, axis=0))
+    slot_of = lax.broadcasted_iota(jnp.int32, (slots_all, row_count), 0) == target[None, :]
+    upstream_slots = jnp.dot(slot_of.astype(bfloat), cotangent, preferred_element_type=single).astype(bfloat)
+    upstream_slots = lax.all_to_all(
+        upstream_slots.reshape(expert_count, capacity, model_width), "expert", split_axis=0, concat_axis=0, tiled=True
+    )
+    inputs = tokens.astype(single)
+    first_stream, saved_one, _ = attention_forward_fast(inputs, norm_gains, attn_qkv, attn_out, count_tile, 0)
+    ffn_out, ffn_normed, ffn_factor = norm_forward(first_stream, norm_gains[1])
+    ffn_low = ffn_out.astype(bfloat)
+    hidden = jnp.dot(ffn_low, ffn_up, preferred_element_type=single)
+    acts_low = gelu_tanh(hidden).astype(bfloat)
+    block_out = first_stream + jnp.dot(acts_low, ffn_down, preferred_element_type=single)
+    second_stream, saved_two, count_tile = attention_forward_fast(
+        block_out, norm_gains, attn_qkv, attn_out, count_tile, 1
+    )
+    moe_in, moe_normed, moe_factor = norm_forward(second_stream, norm_gains[3])
+    logits = jnp.dot(moe_in, router, precision=highest)
+    gates = jax.nn.sigmoid(jnp.sum(logits * one_hot, axis=1))
+    moe_low, moe_grad_low, count_tile, up_stay, up_go, down_stay, down_go = expert_layer(
+        moe_in.astype(bfloat),
+        target,
+        (gates * seq_weight)[:, None],
+        count_tile,
+        upstream_slots,
+        expert_up,
+        expert_down,
+    )
+    counts = count_tile[4, :expert_count]
+    expert_up_part = up_stay.astype(single) + swap(up_go, 1).astype(single)
+    expert_down_part = down_stay.astype(single) + swap(down_go, 1).astype(single)
+    moe_out = moe_low.astype(single)
+    final = second_stream + gates[:, None] * moe_out
+    mean_load = total_tokens / expert_count
+    coef = (counts - mean_load) / mean_load
+    final_grad = cotangent.astype(single) * seq_weight
+    gate_slope = gates * (1.0 - gates)
+    gate_grad = jnp.sum(final_grad * moe_out, axis=1)
+    balance_term = switch * (balance_rate / total_tokens) * jnp.sum(one_hot * coef[None, :], axis=1)
+    logit_grad = (gate_grad + balance_term) * gate_slope
+    routed_grad = logit_grad[:, None] * one_hot
+    moe_in_grad = moe_grad_low.astype(single) + jnp.dot(routed_grad, router.T, precision=highest)
+    router_local = switch * jnp.dot(moe_in.T, routed_grad, precision=highest)
+    norm_grad_two, gain_three = norm_backward(moe_in_grad, moe_normed, moe_factor, norm_gains[3])
+    second_grad = final_grad + norm_grad_two
+    block_grad, gain_two, dqkv_two, dbr_two = attention_backward_fast(
+        second_grad, saved_two, norm_gains, attn_qkv, attn_out, 1
+    )
+    products = ((0, (1,)), (2, (3,)))
+    two = weight_products(
+        products, [saved_two[1], dqkv_two, saved_two[2], dbr_two], "attention_weights_two"
+    )
+    block_grad, two = after(block_grad, two)
+    branch_low = block_grad.astype(bfloat)
+    grad_dense_acts = jnp.dot(branch_low, ffn_down.T, preferred_element_type=single)
+    grad_dense_hidden = gelu_back(hidden, grad_dense_acts).astype(bfloat)
+    ffn_in_grad = jnp.dot(grad_dense_hidden, ffn_up.T, preferred_element_type=single)
+    up_halves = weight_products(((0, (1,)),), [ffn_low, grad_dense_hidden], "ffn_up_weights")
+    down_halves = weight_products(((0, (1,)),), [acts_low, branch_low], "ffn_down_weights")
+    norm_grad_one, gain_one = norm_backward(ffn_in_grad, ffn_normed, ffn_factor, norm_gains[1])
+    first_grad = block_grad + norm_grad_one
+    qkv_two, out_two = sum_y(*two[:2]), sum_y(*two[2:])
+    first_grad, (up_halves, down_halves, qkv_two, out_two) = after(
+        first_grad, (up_halves, down_halves, qkv_two, out_two)
+    )
+    gate_sums = switch * jnp.sum(one_hot * gates[:, None], axis=0)
+    small = jnp.concatenate(
+        [
+            jnp.stack([gain_one, gain_two, gain_three]),
+            router_local.T,
+            jnp.pad(gate_sums, (0, model_width - expert_count))[None],
+        ],
+        axis=0,
+    )
+    small = reduce_small(small)
+    input_grad, gain_zero, dqkv_one, dbr_one = attention_backward_fast(
+        first_grad, saved_one, norm_gains, attn_qkv, attn_out, 0
+    )
+    one = weight_products(
+        products, [saved_one[1], dqkv_one, saved_one[2], dbr_one], "attention_weights_one"
+    )
+    qkv_one, out_one = sum_x(sum_z(sum_y(*one[:2]))), sum_x(sum_z(sum_y(*one[2:])))
+    qkv_two, out_two = sum_x(sum_z(qkv_two)), sum_x(sum_z(out_two))
+    up_part, down_part = sum_x(sum_z(sum_y(*up_halves))), sum_x(sum_z(sum_y(*down_halves)))
+    gain_zero = reduce_small(gain_zero[None])
+    load_balance = jnp.sum(coef * small[3 + expert_count, :expert_count]) * (balance_rate / total_tokens)
+    return (
+        block_out.astype(bfloat),
+        final.astype(bfloat),
+        input_grad,
+        load_balance,
+        jnp.concatenate([gain_zero, small[:3]], axis=0),
+        jnp.stack([qkv_one, qkv_two]),
+        jnp.stack([out_one, out_two]),
+        up_part,
+        down_part,
+        expert_up_part,
+        expert_down_part,
+        small[3 : 3 + expert_count].T,
+    )
+
+
 def solution(mesh):
     in_specs = (
         P(("dp", "expert"), None),
@@ -833,4 +1283,6 @@
         P("expert", "dp", None),
         P(),
     )
+    shape = dict(mesh.shape)
+    body = body_fast if shape["dp"] == 4 and shape["expert"] == 8 else body_any
     return jax.shard_map(body, mesh=mesh, in_specs=in_specs, out_specs=out_specs, check_vma=False)

time: 984 us -> 569 us (0.58)
  waiting for transfers between devices: 494 us -> 119 us
  Pallas kernels: 181 us -> 298 us
  blocking collectives: 86.9 us -> 0 us
  matrix products: 109 us -> 35.5 us
  starting transfers between devices: 18.2 us -> 59.7 us
  local copies, waits for them, and re-layouts: 25.9 us -> 7.96 us
  between operations: 18.2 us -> 5.27 us
    reduce_scatter x6 -> x0, waiting for transfers between devices: 406 us -> none  [the longest x1 132 us: body(): lax.psum_scatter(qkv_local.astype(jnp.bfloat16), 'expert', scatter_dimens...]
    ppermute x0 -> x42, waiting for transfers between devices: none -> 119 us  [swap(): lax.ppermute(array, ('dp', 'expert'), [(i, i ^ step) for i in range(total)])]
    pallas_call x4 -> x9, Pallas kernels: 181 us -> 298 us  [kernel_call(): pl.pallas_call(kernel, out_shape=tuple((jax.ShapeDtypeStruct(*o) for o in...]
    psum x2 -> x0, blocking collectives: 86.9 us -> none  [body(): lax.psum((jnp.sum(one_hot, axis=0), switch * jnp.sum(one_hot * gates[:, N...]
    dot_general x19 -> x8, matrix products: 109 us -> 35.5 us  [the longest x1 8.41 us: body_fast(): hidden = jnp.dot(ffn_low, ffn_up, preferred_element_type=single)]
    psum x1 -> x0, waiting for transfers between devices: 56.2 us -> none  [body(): lax.psum(qkv_part.astype(jnp.bfloat16), 'dp').astype(jnp.float32)]
    ppermute x0 -> x42, starting transfers between devices: none -> 52.3 us  [swap(): lax.ppermute(array, ('dp', 'expert'), [(i, i ^ step) for i in range(total)])]
    all_to_all x4 -> x1, waiting for transfers between devices: 31.5 us -> 0.01 us  [body_fast(): lax.all_to_all(upstream_slots.reshape(expert_count, capacity, model_width...]
  transfers between devices with their start and end apart: 11 -> 43, of which waited for: 10 -> 25; matrix products, arithmetic and copies ran while one was open for 9% -> 8% of each run, Pallas kernels for 0% -> 28%
where the time goes in v2:
time: 569 us; the launch traced here: 561 us
  Pallas kernels  298 us (52%)
  waiting for transfers between devices  119 us (21%)
  starting transfers between devices  59.7 us (10%)
  matrix products  35.5 us (6%)
  other arithmetic  34.9 us (6%)
  local copies, waits for them, and re-layouts  7.96 us (1%)
    pallas_call x9, Pallas kernels, kernel_call(): pl.pallas_call(kernel, out_shape=tuple((jax.ShapeDtypeStruct(*o) for o in...  298 us
    ppermute x42, waiting for transfers between devices, swap(): lax.ppermute(array, ('dp', 'expert'), [(i, i ^ step) for i in range(total)])  119 us
    ppermute x42, starting transfers between devices, swap(): lax.ppermute(array, ('dp', 'expert'), [(i, i ^ step) for i in range(total)])  52.3 us
  transfers between devices with their start and end apart: 43, of which 25 were waited for; matrix products, arithmetic and copies ran while one was open for 8% of the time, Pallas kernels for 28%

profile of v2, /device:TPU:0, one launch (start us, length us, event | category | flops | bytes accessed | tf_op | source)
XLA Modules:
  0.0 560.7 jit_solution(16291347077292237083)
XLA Ops:
  7.0 7.4 %all-to-all-start = ((bf16[8,80,768]{2,1,0:T(8,128)(2,1)}), bf16[8,80,768]{2,1,0:T(8,128)(2,1)S(1)}, u32[]{:S(2)}, u32[]{:S(2)}) async-start(bf16[8,80,768]{2,1,0:T(8,128)(2,1)} %bitcast.8), calls=%async_computation | async-start | bytes 1966080 | tf_op jit(solution)/shard_map/all_to_all | solution.py:1157
  20.6 37.2 %forward_zero.1 = (f32[512,768]{1,0:T(8,128)}, bf16[512,768]{1,0:T(8,128)(2,1)}, bf16[512,768]{1,0:T(8,128)(2,1)}, f32[2,8,512]{2,1,0:T(8,128)}, bf16[3,3,2,512,...) custom-call(f32[512,768]{1,0:T(8,128)} %convert_element_type.337.u_ref, ...), custom_call_target="tpu_custom_call" | custom-call | flops 40000000000 | bytes 12582912 | tf_op jit(solution)/shard_map/forward_zero/pallas_call | solution.py:363
  60.3 8.4 %multiply_convert_fusion = (bf16[512,3072]{1,0:T(8,128)(2,1)S(1)}, f32[512,3072]{1,0:T(8,128)}) fusion(bf16[512,768]{1,0:T(8,128)(2,1)S(1)} %multiply_convert_fusion.1.refs_0_, bf16[768,3072]{1,0:T(8,128)(2,1)} %param.23), kind=kOutput, calls=%fused_computation.9 | convolution fusion | flops 2430074880 | bytes 14942208 | tf_op jit(solution)/shard_map/dot_general | solution.py:1164
  72.8 38.9 %forward_one.1 = (f32[512,768]{1,0:T(8,128)}, bf16[512,768]{1,0:T(8,128)(2,1)}, bf16[512,768]{1,0:T(8,128)(2,1)}, f32[2,8,512]{2,1,0:T(8,128)}, bf16[3,3,2,512,1...) custom-call(f32[512,768]{1,0:T(8,128)} %get-tuple-element.159.u_ref, f32[4,768]{1,0:T(4,128)} %gain_ref.7, ...), custom_call_target="tpu_custom_call" | custom-call | flops 40000000000 | bytes 12582912 | tf_op jit(solution)/shard_map/forward_one/pallas_call | solution.py:363
  119.9 75.7 %experts.1 = (bf16[512,768]{1,0:T(8,128)(2,1)}, bf16[512,768]{1,0:T(8,128)(2,1)}, f32[8,128]{1,0:T(8,128)}, bf16[1,192,3072]{2,1,0:T(8,128)(2,1)}, bf16[1,192,30...) custom-call(bf16[512,768]{1,0:T(8,128)(2,1)} %multiply_convert_fusion.2.rows_ref, ...), custom_call_target="tpu_custom_call" | custom-call | flops 60000002048 | bytes 12582912 | tf_op jit(solution)/shard_map/experts/pallas_call | solution.py:363
  203.4 51.2 %backward_one.1 = (f32[512,768]{1,0:T(8,128)}, f32[1,768]{1,0:T(1,128)}, bf16[512,2304]{1,0:T(8,128)(2,1)}, bf16[512,768]{1,0:T(8,128)(2,1)}) custom-call(f32[512,768]{1,0:T(8,128)} %get-tuple-element.140.dh_ref, f32[512,768]{1,0:T(8,128)} %get-tuple-element.159.u_ref, f32[4,768]{1,0:T(4,128)} %gain_ref.7, bf16[512,768]{1,0:T(8,128)(2,1)} %get-tuple-element.82.o_ref.refs_2_, ...), custom_call_target="tpu_custom_call" | custom-call | flops 60000002048 | bytes 12582912 | tf_op jit(solution)/shard_map/backward_one/pallas_call | solution.py:363
  254.6 11.8 %attention_weights_two.1 = (bf16[4,48,2304]{2,1,0:T(8,128)(2,1)}, bf16[4,48,2304]{2,1,0:T(8,128)(2,1)}, bf16[4,48,768]{2,1,0:T(8,128)(2,1)}, bf16[4,48,768]{2,1,0:T(8,128)(2,1)}) custom-call(bf16[512,768]{1,0:T(8,128)(2,1)} %get-tuple-element.87.refs_0_, bf16[512,2304]{1,0:T(8,128)(2,1)} %get-tuple-element.88.refs_1_, ...), custom_call_target="tpu_custom_call" | custom-call | flops 4831838208 | bytes 12582912 | tf_op jit(solution)/shard_map/attention_weights_two/pallas_call | solution.py:363
  266.6 8.1 %fusion.6.refs_1_ = bf16[512,3072]{1,0:T(8,128)(2,1)S(1)} fusion(f32[512,3072]{1,0:T(8,128)} %get-tuple-element.157, bf16[512,768]{1,0:T(8,128)(2,1)S(1)} %convert_element_type.354.refs_1_, bf16[3072,768]{1,0:T(8,128)(2,1)S(1)} %bitcast.141), kind=kOutput, calls=%fused_computation.8 | convolution fusion | flops 2447376384 | bytes 14942208 | tf_op jit(solution)/shard_map/dot_general | solution.py:1208
  274.7 7.4 %multiply_reduce_fusion.1 = (f32[768]{0:T(1024)S(1)}, f32[512]{0:T(512)S(1)}, f32[512]{0:T(512)S(1)}, f32[512,768]{1,0:T(8,128)}) fusion(f32[512,768]{1,0:T(8,128)S(1)} %copy-done.4, f32[512]{0:T(512)S(1)} %copy-done.30, f32[512]{0:T(512)S(1)} %copy-done.28, f32[768]{0:T(1024)S(1)} %copy-done.26, bf16[512,3072]{1,0:T(8,128)(2,1)S(1)} %fusion.6.refs_1_, ...), kind=kOutput, calls=%fused_computation.22 | convolution fusion | flops 2419063040 | bytes 11024384 | tf_op jit(solution)/shard_map/dot_general | solution.py:1210
  283.2 9.3 %ffn_down_weights.1 = (bf16[4,192,768]{2,1,0:T(8,128)(2,1)}, bf16[4,192,768]{2,1,0:T(8,128)(2,1)}) custom-call(bf16[512,3072]{1,0:T(8,128)(2,1)} %copy-done.40, bf16[512,768]{1,0:T(8,128)(2,1)} %copy-done.20), custom_call_target="tpu_custom_call" | custom-call | flops 4831838208 | bytes 12582912 | tf_op jit(solution)/shard_map/ffn_down_weights/pallas_call | solution.py:363
  292.6 9.9 %ffn_up_weights.1 = (bf16[4,48,3072]{2,1,0:T(8,128)(2,1)}, bf16[4,48,3072]{2,1,0:T(8,128)(2,1)}) custom-call(bf16[512,768]{1,0:T(8,128)(2,1)} %copy-done.18, bf16[512,3072]{1,0:T(8,128)(2,1)} %copy-done.39), custom_call_target="tpu_custom_call" | custom-call | flops 4831838208 | bytes 12582912 | tf_op jit(solution)/shard_map/ffn_up_weights/pallas_call | solution.py:363
  308.0 23.7 %collective-permute-done.4 = f32[12,768]{1,0:T(8,128)S(1)} collective-permute-done((f32[12,768]{1,0:T(8,128)S(1)}, f32[12,768]{1,0:T(8,128)S(1)}, u32[]{:S(2)}, u32[]{:S(2)}) %collective-permute-start.4) | collective-permute-done | bytes 36896 | tf_op jit(solution)/shard_map/ppermute | solution.py:903
  331.7 5.8 %collective-permute-start.5 = (f32[12,768]{1,0:T(8,128)S(1)}, f32[12,768]{1,0:T(8,128)S(1)}, u32[]{:S(2)}, u32[]{:S(2)}) collective-permute-start(f32[12,768]{1,0:T(8,128)S(1)} %add.287), channel_id=1, source_target_pairs={{0,2},{1,3},{2,0},{3,1},{4,6},{5,7},{6,4},{7,5},{8,10},{9,11},{10,... | collective-permute-start | bytes 110600 | tf_op jit(solution)/shard_map/ppermute | solution.py:903
  346.3 52.6 %backward_zero.1 = (f32[512,768]{1,0:T(8,128)}, f32[1,768]{1,0:T(1,128)}, bf16[512,2304]{1,0:T(8,128)(2,1)}, bf16[512,768]{1,0:T(8,128)(2,1)}) custom-call(f32[512,768]{1,0:T(8,128)} %multiply_add_fusion.dh_ref, f32[512,768]{1,0:T(8,128)} %convert_element_type.337.u_ref, f32[4,768]{1,0:T(4,128)} %gain_ref.7, ...), custom_call_target="tpu_custom_call" | custom-call | flops 60000002048 | bytes 12582912 | tf_op jit(solution)/shard_map/backward_zero/pallas_call | solution.py:363
  405.8 5.8 %collective-permute-start.26 = (bf16[2,48,768]{2,1,0:T(8,128)(2,1)S(1)}, bf16[2,48,768]{2,1,0:T(8,128)(2,1)S(1)}, u32[]{:S(2)}, u32[]{:S(2)}) collective-permute-start(bf16[2,48,768]{2,1,0:T(8,128)(2,1)S(1)} %dynamic-slice_bitcast_fusion.8), channel_id=1, source_target_pairs={{0,2},{1,3},{2,0},{3,1},{4,6},{5,7},{6,4},{7,5},{8,10},{9,11},{10,... | collective-permute-start | bytes 442376 | tf_op jit(solution)/shard_map/ppermute | solution.py:903
  413.9 11.7 %attention_weights_one.1 = (bf16[4,48,2304]{2,1,0:T(8,128)(2,1)}, bf16[4,48,2304]{2,1,0:T(8,128)(2,1)}, bf16[4,48,768]{2,1,0:T(8,128)(2,1)}, bf16[4,48,768]{2,1,0:T(8,128)(2,1)}) custom-call(bf16[512,768]{1,0:T(8,128)(2,1)} %get-tuple-element.111.refs_0_, bf16[512,2304]{1,0:T(8,128)(2,1)} %get-tuple-element.112.refs_1_, ...), custom_call_target="tpu_custom_call" | custom-call | flops 4831838208 | bytes 12582912 | tf_op jit(solution)/shard_map/attention_weights_one/pallas_call | solution.py:363
  456.5 4.3 collective-permute-done.23
  465.3 6.7 %collective-permute-done.18 = bf16[48,2304]{1,0:T(8,128)(2,1)S(1)} collective-permute-done((bf16[48,2304]{1,0:T(8,128)(2,1)S(1)}, bf16[48,2304]{1,0:T(8,128)(2,1)S(1)}, u32[]{:S(2)}, u32[]{:S(2)}) %collective-permute-start.18) | collective-permute-done | bytes 221216 | tf_op jit(solution)/shard_map/ppermute | solution.py:903
  479.8 6.4 %collective-permute-done.30 = bf16[4,48,3072]{2,1,0:T(8,128)(2,1)S(1)} collective-permute-done((bf16[4,48,3072]{2,1,0:T(8,128)(2,1)S(1)}, bf16[4,48,3072]{2,1,0:T(8,128)(2,1)S(1)}, u32[]{:S(2)}, u32[]{:S(2)}) %collective-permute-start.30) | collective-permute-done | bytes 1179680 | tf_op jit(solution)/shard_map/ppermute | solution.py:903
  486.6 4.5 collective-permute-done.13
  495.3 8.8 %collective-permute-done.14 = bf16[48,2304]{1,0:T(8,128)(2,1)S(1)} collective-permute-done((bf16[48,2304]{1,0:T(8,128)(2,1)S(1)}, bf16[48,2304]{1,0:T(8,128)(2,1)S(1)}, u32[]{:S(2)}, u32[]{:S(2)}) %collective-permute-start.14) | collective-permute-done | bytes 221216 | tf_op jit(solution)/shard_map/ppermute | solution.py:903
  514.4 17.0 %collective-permute-done.36 = bf16[2,192,768]{2,1,0:T(8,128)(2,1)S(1)} collective-permute-done((bf16[2,192,768]{2,1,0:T(8,128)(2,1)S(1)}, bf16[2,192,768]{2,1,0:T(8,128)(2,1)S(1)}, u32[]{:S(2)}, u32[]{:S(2)}) %collective-permute-start.36) | collective-permute-done | bytes 589856 | tf_op jit(solution)/shard_map/ppermute | solution.py:903
  533.6 12.5 %collective-permute-done.37 = bf16[192,768]{1,0:T(8,128)(2,1)S(1)} collective-permute-done((bf16[192,768]{1,0:T(8,128)(2,1)S(1)}, bf16[192,768]{1,0:T(8,128)(2,1)S(1)}, u32[]{:S(2)}, u32[]{:S(2)}) %collective-permute-start.37) | collective-permute-done | bytes 294944 | tf_op jit(solution)/shard_map/ppermute | solution.py:903
  549.2 5.9 %collective-permute-done.38 = bf16[192,768]{1,0:T(8,128)(2,1)S(1)} collective-permute-done((bf16[192,768]{1,0:T(8,128)(2,1)S(1)}, bf16[192,768]{1,0:T(8,128)(2,1)S(1)}, u32[]{:S(2)}, u32[]{:S(2)}) %collective-permute-start.38) | collective-permute-done | bytes 294944 | tf_op jit(solution)/shard_map/ppermute | solution.py:903
  (287 shorter events, 124.5 us)
Async XLA Ops:
  7.0 112.0 %all-to-all-start = ((bf16[8,80,768]{2,1,0:T(8,128)(2,1)}), bf16[8,80,768]{2,1,0:T(8,128)(2,1)S(1)}, u32[]{:S(2)}, u32[]{:S(2)}) async-start(bf16[8,80,768]{2,1,0:T(8,128)(2,1)} %bitcast.8), calls=%async_computation | async-start | bytes 1966080 | tf_op jit(solution)/shard_map/all_to_all | solution.py:1157
  282.7 9.7 %collective-permute-start.2 = (f32[12,768]{1,0:T(8,128)S(1)}, f32[12,768]{1,0:T(8,128)S(1)}, u32[]{:S(2)}, u32[]{:S(2)}) collective-permute-start(f32[12,768]{1,0:T(8,128)S(1)} %concatenate.36), channel_id=1, source_target_pairs={{0,8},{1,9},{2,10},{3,11},{4,12},{5,13},{6,14},{7,15},{8,0},{9,1},... | collective-permute-start | bytes 110600 | tf_op jit(solution)/shard_map/ppermute | solution.py:903
  292.5 14.2 %collective-permute-start.3 = (f32[12,768]{1,0:T(8,128)S(1)}, f32[12,768]{1,0:T(8,128)S(1)}, u32[]{:S(2)}, u32[]{:S(2)}) collective-permute-start(f32[12,768]{1,0:T(8,128)S(1)} %add.285), channel_id=1, source_target_pairs={{0,16},{1,17},{2,18},{3,19},{4,20},{5,21},{6,22},{7,23},{8,24},{9,... | collective-permute-start | bytes 110600 | tf_op jit(solution)/shard_map/ppermute | solution.py:903
  302.6 42.8 %collective-permute-start.1 = (bf16[4,48,768]{2,1,0:T(8,128)(2,1)S(1)}, bf16[4,48,768]{2,1,0:T(8,128)(2,1)S(1)}, u32[]{:S(2)}, u32[]{:S(2)}) collective-permute-start(bf16[4,48,768]{2,1,0:T(8,128)(2,1)S(1)} %copy-done.36), channel_id=1, source_target_pairs={{0,1},{1,0},{2,3},{3,2},{4,5},{5,4},{6,7},{7,6},{8,9},{9,8},{10,11... | collective-permute-start | bytes 884744 | tf_op jit(solution)/shard_map/ppermute | solution.py:903
  303.9 41.5 %collective-permute-start = (bf16[4,48,2304]{2,1,0:T(8,128)(2,1)S(1)}, bf16[4,48,2304]{2,1,0:T(8,128)(2,1)S(1)}, u32[]{:S(2)}, u32[]{:S(2)}) collective-permute-start(bf16[4,48,2304]{2,1,0:T(8,128)(2,1)S(1)} %copy-done.35), channel_id=1, source_target_pairs={{0,1},{1,0},{2,3},{3,2},{4,5},{5,4},{6,7},{7,6},{8,9},{9,8},{10,11... | collective-permute-start | bytes 2654216 | tf_op jit(solution)/shard_map/ppermute | solution.py:903
  304.6 134.9 %collective-permute-start.40 = (bf16[1,192,3072]{2,1,0:T(8,128)(2,1)}, bf16[1,192,3072]{2,1,0:T(8,128)(2,1)}, u32[]{:S(2)}, u32[]{:S(2)}) collective-permute-start(bf16[1,192,3072]{2,1,0:T(8,128)(2,1)} %get-tuple-element.125), channel_id=1, source_target_pairs={{0,16},{1,17},{2,18},{3,19},{4,20},{5,21},{6,22},{7,23},{8,24},{9,... | collective-permute-start | bytes 3538952 | tf_op jit(solution)/shard_map/ppermute | solution.py:903
  306.5 136.9 %collective-permute-start.41 = (bf16[1,768,768]{2,1,0:T(8,128)(2,1)}, bf16[1,768,768]{2,1,0:T(8,128)(2,1)}, u32[]{:S(2)}, u32[]{:S(2)}) collective-permute-start(bf16[1,768,768]{2,1,0:T(8,128)(2,1)} %get-tuple-element.127), channel_id=1, source_target_pairs={{0,16},{1,17},{2,18},{3,19},{4,20},{5,21},{6,22},{7,23},{8,24},{9,... | collective-permute-start | bytes 3538952 | tf_op jit(solution)/shard_map/ppermute | solution.py:903
  306.7 25.0 %collective-permute-start.4 = (f32[12,768]{1,0:T(8,128)S(1)}, f32[12,768]{1,0:T(8,128)S(1)}, u32[]{:S(2)}, u32[]{:S(2)}) collective-permute-start(f32[12,768]{1,0:T(8,128)S(1)} %add.286), channel_id=1, source_target_pairs={{0,1},{1,0},{2,3},{3,2},{4,5},{5,4},{6,7},{7,6},{8,9},{9,8},{10,11... | collective-permute-start | bytes 110600 | tf_op jit(solution)/shard_map/ppermute | solution.py:903
  405.8 21.5 %collective-permute-start.26 = (bf16[2,48,768]{2,1,0:T(8,128)(2,1)S(1)}, bf16[2,48,768]{2,1,0:T(8,128)(2,1)S(1)}, u32[]{:S(2)}, u32[]{:S(2)}) collective-permute-start(bf16[2,48,768]{2,1,0:T(8,128)(2,1)S(1)} %dynamic-slice_bitcast_fusion.8), channel_id=1, source_target_pairs={{0,2},{1,3},{2,0},{3,1},{4,6},{5,7},{6,4},{7,5},{8,10},{9,11},{10,... | collective-permute-start | bytes 442376 | tf_op jit(solution)/shard_map/ppermute | solution.py:903
  411.6 14.0 %collective-permute-start.10 = (f32[1,768]{1,0:T(1,128)S(1)}, f32[1,768]{1,0:T(1,128)S(1)}, u32[]{:S(2)}, u32[]{:S(2)}) collective-permute-start(f32[1,768]{1,0:T(1,128)S(1)} %add.292), channel_id=1, source_target_pairs={{0,2},{1,3},{2,0},{3,1},{4,6},{5,7},{6,4},{7,5},{8,10},{9,11},{10,... | collective-permute-start | bytes 9224 | tf_op jit(solution)/shard_map/ppermute | solution.py:903
  428.8 27.5 %collective-permute-start.17 = (bf16[2,48,2304]{2,1,0:T(8,128)(2,1)S(1)}, bf16[2,48,2304]{2,1,0:T(8,128)(2,1)S(1)}, u32[]{:S(2)}, u32[]{:S(2)}) collective-permute-start(bf16[2,48,2304]{2,1,0:T(8,128)(2,1)S(1)} %dynamic-slice_bitcast_fusion.2), channel_id=1, source_target_pairs={{0,2},{1,3},{2,0},{3,1},{4,6},{5,7},{6,4},{7,5},{8,10},{9,11},{10,... | collective-permute-start | bytes 1327112 | tf_op jit(solution)/shard_map/ppermute | solution.py:903
  430.2 17.6 %collective-permute-start.21 = (bf16[4,48,768]{2,1,0:T(8,128)(2,1)}, bf16[4,48,768]{2,1,0:T(8,128)(2,1)S(1)}, u32[]{:S(2)}, u32[]{:S(2)}) collective-permute-start(bf16[4,48,768]{2,1,0:T(8,128)(2,1)} %get-tuple-element.118), channel_id=1, source_target_pairs={{0,1},{1,0},{2,3},{3,2},{4,5},{5,4},{6,7},{7,6},{8,9},{9,8},{10,11... | collective-permute-start | bytes 884744 | tf_op jit(solution)/shard_map/ppermute | solution.py:903
  438.2 40.1 %collective-permute-start.12 = (bf16[4,48,2304]{2,1,0:T(8,128)(2,1)}, bf16[4,48,2304]{2,1,0:T(8,128)(2,1)S(1)}, u32[]{:S(2)}, u32[]{:S(2)}) collective-permute-start(bf16[4,48,2304]{2,1,0:T(8,128)(2,1)} %get-tuple-element.115), channel_id=1, source_target_pairs={{0,1},{1,0},{2,3},{3,2},{4,5},{5,4},{6,7},{7,6},{8,9},{9,8},{10,11... | collective-permute-start | bytes 2654216 | tf_op jit(solution)/shard_map/ppermute | solution.py:903
  439.5 46.7 %collective-permute-start.30 = (bf16[4,48,3072]{2,1,0:T(8,128)(2,1)S(1)}, bf16[4,48,3072]{2,1,0:T(8,128)(2,1)S(1)}, u32[]{:S(2)}, u32[]{:S(2)}) collective-permute-start(bf16[4,48,3072]{2,1,0:T(8,128)(2,1)S(1)} %copy-done.34), channel_id=1, source_target_pairs={{0,1},{1,0},{2,3},{3,2},{4,5},{5,4},{6,7},{7,6},{8,9},{9,8},{10,11... | collective-permute-start | bytes 3538952 | tf_op jit(solution)/shard_map/ppermute | solution.py:903
  443.4 64.6 %collective-permute-start.35 = (bf16[4,192,768]{2,1,0:T(8,128)(2,1)S(1)}, bf16[4,192,768]{2,1,0:T(8,128)(2,1)S(1)}, u32[]{:S(2)}, u32[]{:S(2)}) collective-permute-start(bf16[4,192,768]{2,1,0:T(8,128)(2,1)S(1)} %copy-done.33), channel_id=1, source_target_pairs={{0,1},{1,0},{2,3},{3,2},{4,5},{5,4},{6,7},{7,6},{8,9},{9,8},{10,11... | collective-permute-start | bytes 3538952 | tf_op jit(solution)/shard_map/ppermute | solution.py:903
  461.3 10.7 %collective-permute-start.18 = (bf16[48,2304]{1,0:T(8,128)(2,1)S(1)}, bf16[48,2304]{1,0:T(8,128)(2,1)S(1)}, u32[]{:S(2)}, u32[]{:S(2)}) collective-permute-start(bf16[48,2304]{1,0:T(8,128)(2,1)S(1)} %dynamic-slice_bitcast_fusion.6), channel_id=1, source_target_pairs={{0,4},{1,5},{2,6},{3,7},{4,0},{5,1},{6,2},{7,3},{8,12},{9,13},{10,... | collective-permute-start | bytes 663560 | tf_op jit(solution)/shard_map/ppermute | solution.py:903
  478.5 12.6 %collective-permute-start.13 = (bf16[2,48,2304]{2,1,0:T(8,128)(2,1)S(1)}, bf16[2,48,2304]{2,1,0:T(8,128)(2,1)S(1)}, u32[]{:S(2)}, u32[]{:S(2)}) collective-permute-start(bf16[2,48,2304]{2,1,0:T(8,128)(2,1)S(1)} %dynamic-slice_bitcast_fusion.3), channel_id=1, source_target_pairs={{0,2},{1,3},{2,0},{3,1},{4,6},{5,7},{6,4},{7,5},{8,10},{9,11},{10,... | collective-permute-start | bytes 1327112 | tf_op jit(solution)/shard_map/ppermute | solution.py:903
  491.3 12.8 %collective-permute-start.14 = (bf16[48,2304]{1,0:T(8,128)(2,1)S(1)}, bf16[48,2304]{1,0:T(8,128)(2,1)S(1)}, u32[]{:S(2)}, u32[]{:S(2)}) collective-permute-start(bf16[48,2304]{1,0:T(8,128)(2,1)S(1)} %dynamic-slice_bitcast_fusion.7), channel_id=1, source_target_pairs={{0,4},{1,5},{2,6},{3,7},{4,0},{5,1},{6,2},{7,3},{8,12},{9,13},{10,... | collective-permute-start | bytes 663560 | tf_op jit(solution)/shard_map/ppermute | solution.py:903
  493.5 20.3 %collective-permute-start.31 = (bf16[2,48,3072]{2,1,0:T(8,128)(2,1)S(1)}, bf16[2,48,3072]{2,1,0:T(8,128)(2,1)S(1)}, u32[]{:S(2)}, u32[]{:S(2)}) collective-permute-start(bf16[2,48,3072]{2,1,0:T(8,128)(2,1)S(1)} %dynamic-slice_bitcast_fusion.1), channel_id=1, source_target_pairs={{0,2},{1,3},{2,0},{3,1},{4,6},{5,7},{6,4},{7,5},{8,10},{9,11},{10,... | collective-permute-start | bytes 1769480 | tf_op jit(solution)/shard_map/ppermute | solution.py:903
  508.4 22.9 %collective-permute-start.36 = (bf16[2,192,768]{2,1,0:T(8,128)(2,1)S(1)}, bf16[2,192,768]{2,1,0:T(8,128)(2,1)S(1)}, u32[]{:S(2)}, u32[]{:S(2)}) collective-permute-start(bf16[2,192,768]{2,1,0:T(8,128)(2,1)S(1)} %dynamic-slice_bitcast_fusion), channel_id=1, source_target_pairs={{0,2},{1,3},{2,0},{3,1},{4,6},{5,7},{6,4},{7,5},{8,10},{9,11},{10,... | collective-permute-start | bytes 1769480 | tf_op jit(solution)/shard_map/ppermute | solution.py:903
  510.9 20.8 %collective-permute-start.16 = (bf16[48,2304]{1,0:T(8,128)(2,1)S(1)}, bf16[48,2304]{1,0:T(8,128)(2,1)S(1)}, u32[]{:S(2)}, u32[]{:S(2)}) collective-permute-start(bf16[48,2304]{1,0:T(8,128)(2,1)S(1)} %add_convert_fusion.9), channel_id=1, source_target_pairs={{0,8},{1,9},{2,10},{3,11},{4,12},{5,13},{6,14},{7,15},{8,0},{9,1},... | collective-permute-start | bytes 663560 | tf_op jit(solution)/shard_map/ppermute | solution.py:903
  514.0 17.8 %collective-permute-start.32 = (bf16[48,3072]{1,0:T(8,128)(2,1)S(1)}, bf16[48,3072]{1,0:T(8,128)(2,1)S(1)}, u32[]{:S(2)}, u32[]{:S(2)}) collective-permute-start(bf16[48,3072]{1,0:T(8,128)(2,1)S(1)} %dynamic-slice_bitcast_fusion.5), channel_id=1, source_target_pairs={{0,4},{1,5},{2,6},{3,7},{4,0},{5,1},{6,2},{7,3},{8,12},{9,13},{10,... | collective-permute-start | bytes 884744 | tf_op jit(solution)/shard_map/ppermute | solution.py:903
  531.6 14.4 %collective-permute-start.37 = (bf16[192,768]{1,0:T(8,128)(2,1)S(1)}, bf16[192,768]{1,0:T(8,128)(2,1)S(1)}, u32[]{:S(2)}, u32[]{:S(2)}) collective-permute-start(bf16[192,768]{1,0:T(8,128)(2,1)S(1)} %dynamic-slice_bitcast_fusion.4), channel_id=1, source_target_pairs={{0,4},{1,5},{2,6},{3,7},{4,0},{5,1},{6,2},{7,3},{8,12},{9,13},{10,... | collective-permute-start | bytes 884744 | tf_op jit(solution)/shard_map/ppermute | solution.py:903
  531.9 15.8 %collective-permute-start.33 = (bf16[48,3072]{1,0:T(8,128)(2,1)S(1)}, bf16[48,3072]{1,0:T(8,128)(2,1)S(1)}, u32[]{:S(2)}, u32[]{:S(2)}) collective-permute-start(bf16[48,3072]{1,0:T(8,128)(2,1)S(1)} %fusion.31), channel_id=1, source_target_pairs={{0,16},{1,17},{2,18},{3,19},{4,20},{5,21},{6,22},{7,23},{8,24},{9,... | collective-permute-start | bytes 884744 | tf_op jit(solution)/shard_map/ppermute | solution.py:903
  (65 other events, 759.8 us)
